TPU v7x, 32 devices: a whole 2x2x4 slice. The times are simulated.
32 devices in a mesh: sys: 2 (over x), slab: 16 (over z, y, core).
Axes of the slice: x: 2, y: 2, z: 4, core: 2. Of those that a mesh axis runs over, the one named last changes fastest.
Arguments:
- correlation: float32 [24, 256, 32, 256], P('sys', 'slab'), parts along dimension 0, may hold values from -6 to 6
- lj_field: float32 [12, 256, 32, 256], P('sys', 'slab'), parts along dimension 0, may hold values from -1 to 3
- potential: float32 [512, 32, 256], P(('sys', 'slab')), parts along dimension 0, may hold values from -8 to 8
- species: int32 [12], replicated, may hold values from 0 to 5
- charges: int32 [12], replicated, may hold values from -2 to 2
- chi_amp: float32 [3, 12, 12], replicated, may hold values from -2.4 to 2.4
- chi_width: float32 [3], replicated, may hold values from 0.05 to 2
Outputs:
- total_corr: float32 [24, 256, 32, 256], P('sys', 'slab'), parts along dimension 0
- next_corr: float32 [24, 256, 32, 256], P('sys', 'slab'), parts along dimension 0
- residual_rms: float32 [2], P('sys'), parts along dimension 0
There are 2 independent parts, one for each index of `sys`. A program takes and returns all parts, laid end to end along the dimension named above; an argument that names none is the same for every part. Nothing has to cross between parts.
All inputs are finite; a program needn't handle non-finite values.
Results may differ from a plain program's by a relative error of at most 0.0003.
Values sent between devices are 32-bit elements; how exact they have to be, the bound alone decides.
A program may use at most 320 MiB of HBM per device.

v0:
```python
import math

import jax
import jax.numpy as jnp
from jax import lax
from jax.sharding import PartitionSpec as P

precise = lax.Precision.HIGHEST
full_turn = 2.0 * math.pi


def angle_table(period, height, breadth):
    product = (
        lax.broadcasted_iota(jnp.int32, (height, breadth), 0)
        * lax.broadcasted_iota(jnp.int32, (height, breadth), 1)
        % period
    )
    theta = product.astype(jnp.float32) * (full_turn / period)
    return (jnp.cos(theta), jnp.sin(theta))


def dft_last(real_part, imag_part, direction):
    length = real_part.shape[-1]
    outer_len = 1 << length.bit_length() // 2
    inner_len = length // outer_len
    leading = real_part.shape[:-1]
    real_in = real_part.reshape(leading + (outer_len, inner_len))
    imag_in = imag_part.reshape(leading + (outer_len, inner_len))
    outer_cos, outer_sin = angle_table(outer_len, outer_len, outer_len)

    def outer_apply(values, factors):
        return jnp.einsum("...ab,ac->...cb", values, factors, precision=precise)

    step_real = outer_apply(real_in, outer_cos) - direction * outer_apply(imag_in, outer_sin)
    step_imag = outer_apply(imag_in, outer_cos) + direction * outer_apply(real_in, outer_sin)
    twist_cos, twist_sin = angle_table(length, outer_len, inner_len)
    turned_real = step_real * twist_cos - direction * step_imag * twist_sin
    turned_imag = step_imag * twist_cos + direction * step_real * twist_sin
    inner_cos, inner_sin = angle_table(inner_len, inner_len, inner_len)

    def inner_apply(values, factors):
        return jnp.einsum("...cb,bd->...dc", values, factors, precision=precise)

    out_real = inner_apply(turned_real, inner_cos) - direction * inner_apply(turned_imag, inner_sin)
    out_imag = inner_apply(turned_imag, inner_cos) + direction * inner_apply(turned_real, inner_sin)
    return (out_real.reshape(leading + (length,)), out_imag.reshape(leading + (length,)))


def dft_along(real_part, imag_part, axis, direction):
    moved_real = jnp.moveaxis(real_part, axis, -1)
    moved_imag = jnp.moveaxis(imag_part, axis, -1)
    out_real, out_imag = dft_last(moved_real, moved_imag, direction)
    return (jnp.moveaxis(out_real, -1, axis), jnp.moveaxis(out_imag, -1, axis))


def signed_freq(index, total):
    return ((index + total // 2) % total - total // 2).astype(jnp.float32) / total


def wave_square(column_ids, depth, extent, columns):
    along_b = signed_freq(column_ids, columns)[:, None, None]
    along_z = signed_freq(jnp.arange(depth), depth)[None, :, None]
    along_a = signed_freq(jnp.arange(extent), extent)[None, None, :]
    return full_turn * full_turn * (along_a * along_a + along_z * along_z + along_b * along_b)


def mix_sites(real_part, imag_part, ksquare, chi_amp, chi_width):
    weight = jnp.exp(-chi_width.reshape((-1,) + (1,) * ksquare.ndim) * ksquare[None])
    stacked = jnp.stack((real_part, imag_part))
    scaled = weight[:, None, None] * stacked[None]
    mixed = jnp.einsum("mab,mcb...->ca...", chi_amp, scaled, precision=precise)
    return (real_part + mixed[0], imag_part + mixed[1])


def to_spectrum(pieces):
    real_part = jnp.transpose(pieces[0], (0, 3, 2, 1))
    imag_part = jnp.transpose(pieces[1], (0, 3, 2, 1))
    real_part, imag_part = dft_last(real_part, imag_part, -1.0)
    return dft_along(real_part, imag_part, 2, -1.0)


def body(correlation, lj_field, potential, species, charges, chi_amp, chi_width):
    site_count = correlation.shape[0]
    local_rows = correlation.shape[1]
    depth = correlation.shape[2]
    columns = correlation.shape[3]
    half_cols = columns // 2
    devices = lax.axis_size("slab")
    my_index = lax.axis_index("slab")
    flat = correlation.reshape(-1, columns)
    sample_ids = jnp.arange(columns)
    parity = (1 - 2 * (sample_ids % 2)).astype(jnp.float32)
    fwd_cos, fwd_sin = angle_table(columns, columns, half_cols)
    fwd_sin = jnp.where(jnp.arange(half_cols)[None, :] == 0, -parity[:, None], fwd_sin)
    spec_real = jnp.dot(flat, fwd_cos, precision=precise).reshape(
        site_count, local_rows, depth, half_cols
    )
    spec_imag = -jnp.dot(flat, fwd_sin, precision=precise).reshape(
        site_count, local_rows, depth, half_cols
    )
    spec_real, spec_imag = to_spectrum(
        (
            lax.all_to_all(spec_real, "slab", split_axis=3, concat_axis=1, tiled=True),
            lax.all_to_all(spec_imag, "slab", split_axis=3, concat_axis=1, tiled=True),
        )
    )
    extent = spec_real.shape[3]
    local_cols = spec_real.shape[1]
    column_ids = my_index * local_cols + jnp.arange(local_cols)
    ksquare = wave_square(column_ids, depth, extent, columns)
    mixed_real, mixed_imag = mix_sites(spec_real, spec_imag, ksquare, chi_amp, chi_width)
    inverse_scale = 1.0 / (extent * depth * columns)
    col_real = spec_real[:, 0]
    col_imag = spec_imag[:, 0]
    rev_real = jnp.roll(jnp.flip(col_real, (1, 2)), (1, 1), axis=(1, 2))
    rev_imag = jnp.roll(jnp.flip(col_imag, (1, 2)), (1, 1), axis=(1, 2))
    even_real = 0.5 * (col_real + rev_real)
    even_imag = 0.5 * (col_imag - rev_imag)
    upper_real = 0.5 * (col_imag + rev_imag)
    upper_imag = -0.5 * (col_real - rev_real)
    zero_square = wave_square(jnp.zeros((1,), jnp.int32), depth, extent, columns)[0]
    upper_square = wave_square(jnp.full((1,), half_cols, jnp.int32), depth, extent, columns)[0]
    even_real, even_imag = mix_sites(even_real, even_imag, zero_square, chi_amp, chi_width)
    upper_real, upper_imag = mix_sites(upper_real, upper_imag, upper_square, chi_amp, chi_width)
    packed_real = even_real - upper_imag
    packed_imag = even_imag + upper_real
    special = ((jnp.arange(local_cols) == 0) & (my_index == 0))[None, :, None, None]
    mixed_real = jnp.where(special, packed_real[:, None], mixed_real)
    mixed_imag = jnp.where(special, packed_imag[:, None], mixed_imag)
    inv_cos, inv_sin = angle_table(columns, half_cols, columns)
    first_row = jnp.arange(half_cols)[:, None] == 0
    inv_cos = jnp.where(first_row, 1.0, 2.0 * inv_cos)
    inv_sin = jnp.where(first_row, -parity[None, :], 2.0 * inv_sin)
    inv_table = jnp.concatenate((inv_cos, -inv_sin), axis=0) * inverse_scale
    back_real, back_imag = dft_last(mixed_real, mixed_imag, 1.0)
    back_real, back_imag = dft_along(back_real, back_imag, 2, 1.0)
    part_real = jnp.transpose(
        lax.all_to_all(back_real, "slab", split_axis=3, concat_axis=1, tiled=True), (0, 3, 2, 1)
    )
    part_imag = jnp.transpose(
        lax.all_to_all(back_imag, "slab", split_axis=3, concat_axis=1, tiled=True), (0, 3, 2, 1)
    )
    count = part_real.shape[-1]
    shaped = part_real.shape[:-1] + (columns,)
    joined = jnp.concatenate((part_real, part_imag), axis=-1).reshape(-1, 2 * count)
    total_corr = jnp.dot(joined, inv_table, precision=precise).reshape(shaped)
    indirect = total_corr - correlation
    onehot = (species[:, None] == jnp.arange(lj_field.shape[0])[None, :]).astype(jnp.float32)
    energy = jnp.einsum("sk,kxyz->sxyz", onehot, lj_field, precision=precise)
    energy = energy + charges.astype(jnp.float32)[:, None, None, None] * potential[None]
    shifted = indirect - energy
    next_corr = jnp.where(shifted < 0, jnp.expm1(jnp.minimum(shifted, 0.0)), shifted) - indirect
    change = next_corr - correlation
    summed_sq = lax.psum(jnp.sum(change * change), "slab")
    cells = site_count * local_rows * devices * depth * columns
    residual_rms = jnp.sqrt(summed_sq / cells + 1e-06).reshape(1)
    return (total_corr, next_corr, residual_rms)


def solution(mesh):
    placed = (
        P("sys", "slab", None, None),
        P("sys", "slab", None, None),
        P(("sys", "slab"), None, None),
        P(),
        P(),
        P(),
        P(),
    )
    return jax.shard_map(
        body,
        mesh=mesh,
        in_specs=placed,
        out_specs=(P("sys", "slab", None, None), P("sys", "slab", None, None), P("sys")),
        check_vma=False,
    )
```

profile of v0, /device:TPU:0, one launch (start us, length us, event | category | flops | bytes accessed | tf_op | source)
XLA Modules:
  0.0 1105.1 jit_solution(15128511944465025334)
XLA Ops:
  1.2 11.8 %fusion.36 = f32[6144,128]{0,1:T(8,128)} fusion(f32[6144,256]{1,0:T(8,128)} %bitcast.335, f32[256]{0:T(256)S(1)} %fusion.260, pred[128]{0:T(512)(128)(4,1)S(1)} %iota_compare_fusion.1), kind=kOutput, calls=%fused_computation.49 | convolution fusion | flops 2417197056 | bytes 9438336 | tf_op jit(solution)/shard_map/dot_general | solution.py:98
  16.6 11.4 %copy.184 = f32[12,16,32,128]{2,1,0,3:T(8,128)} copy(f32[12,16,32,128]{3,2,1,0:T(8,128)} %bitcast.369) | data formatting | bytes 6291456 | tf_op jit(solution)/shard_map/neg | solution.py:98
  28.0 14.1 %reshape.539 = f32[16,1,49152]{2,1,0:T(1,128)} reshape(f32[128,12,16,32]{3,2,1,0:T(8,128)} %bitcast.345) | data formatting | bytes 6291456
  49.8 11.5 %convolution_bitcast_fusion = f32[6144,128]{0,1:T(8,128)} fusion(f32[6144,256]{1,0:T(8,128)} %bitcast.336), kind=kOutput, calls=%fused_computation.50 | convolution fusion | flops 2416377856 | bytes 9437184 | tf_op jit(solution)/shard_map/dot_general | solution.py:95
  64.8 11.4 %copy.178 = f32[12,16,32,128]{2,1,0,3:T(8,128)} copy(f32[12,16,32,128]{3,2,1,0:T(8,128)} %bitcast.370) | data formatting | bytes 6291456 | tf_op jit(solution)/shard_map/reshape | solution.py:95
  76.2 14.1 %reshape.537 = f32[16,1,49152]{2,1,0:T(1,128)} reshape(f32[128,12,16,32]{3,2,1,0:T(8,128)} %bitcast.346) | data formatting | bytes 6291456
  90.3 18.9 %all-to-all-done.1 = f32[16,1,49152]{2,1,0:T(1,128)} async-done(((f32[16,1,49152]{2,1,0:T(1,128)}), f32[16,1,49152]{2,1,0:T(1,128)}, u32[]{:S(2)}, u32[]{:S(2)}) %all-to-all-start.1) | async-done | bytes 3145760 | tf_op jit(solution)/shard_map/all_to_all | solution.py:104
  109.2 15.9 %all-to-all-start = ((f32[16,1,49152]{2,1,0:T(1,128)}), f32[16,1,49152]{2,1,0:T(1,128)}, u32[]{:S(2)}, u32[]{:S(2)}) async-start(f32[16,1,49152]{2,1,0:T(1,128)} %reshape.537), calls=%async_computation | async-start | bytes 6291456 | tf_op jit(solution)/shard_map/all_to_all | solution.py:103
  130.0 11.8 %reduce = f32[16,49152]{1,0:T(8,128)} reduce(f32[16,1,49152]{2,1,0:T(1,128)} %all-to-all-done.1, f32[]{:T(128)} %broadcast.918), dimensions={1}, to_apply=%all_to_all.56.reduce_sub_computation | reduce | bytes 6291460 | tf_op jit(solution)/shard_map/all_to_all | solution.py:104
  141.8 12.3 %reshape.540 = f32[128,12,16,32]{3,2,1,0:T(8,128)} reshape(f32[16,49152]{1,0:T(8,128)} %reduce) | data formatting | bytes 6291456
  154.1 24.5 %fusion.4 = f32[16,12,8,32,16]{3,0,4,2,1:T(8,128)} fusion(f32[12,8,32,16,16]{2,4,0,1,3:T(8,128)} %bitcast.333), kind=kOutput, calls=%fused_computation.15 | convolution fusion | flops 150998528 | bytes 6291456 | tf_op jit(solution)/shard_map/...ab,ac->...cb/dot_general | solution.py:32
  178.6 17.6 %fusion.6 = f32[16,12,8,32,16]{3,0,4,2,1:T(8,128)} fusion(f32[12,8,32,16,16]{2,4,0,1,3:T(8,128)S(1)} %bitcast.334), kind=kOutput, calls=%fused_computation.17 | convolution fusion | flops 150998528 | bytes 6291456 | tf_op jit(solution)/shard_map/...ab,ac->...cb/dot_general | solution.py:32
  196.2 11.8 %reduce.1 = f32[16,49152]{1,0:T(8,128)} reduce(f32[16,1,49152]{2,1,0:T(1,128)} %all-to-all-done, f32[]{:T(128)} %broadcast.918), dimensions={1}, to_apply=%all_to_all.52.reduce_sub_computation | reduce | bytes 6291460 | tf_op jit(solution)/shard_map/all_to_all | solution.py:103
  208.0 12.3 %reshape.538 = f32[128,12,16,32]{3,2,1,0:T(8,128)} reshape(f32[16,49152]{1,0:T(8,128)} %reduce.1) | data formatting | bytes 6291456
  220.3 24.6 %fusion.8 = f32[16,12,8,32,16]{3,0,4,2,1:T(8,128)} fusion(f32[12,8,32,16,16]{2,4,0,1,3:T(8,128)} %bitcast.327), kind=kOutput, calls=%fused_computation.19 | convolution fusion | flops 150998528 | bytes 6291456 | tf_op jit(solution)/shard_map/...ab,ac->...cb/dot_general | solution.py:32
  245.0 33.6 %subtract_bitcast_fusion.3 = (f32[12,8,32,16,16]{2,3,4,1,0:T(8,128)}, f32[12,8,32,16,16]{2,3,4,1,0:T(8,128)}) fusion(f32[16,16]{0,1:T(8,128)S(1)} %get-tuple-element.33, f32[16,16]{0,1:T(8,128)S(1)} %get-tuple-element.34, f32[16,12,8,32,16]{3,0,4,2,1:T(8,128)} %fusion.6, f32[16,12,8,32,16]{3,0,4,2,1:T(8,128)} %fusion.4, f32[16,12,8,32,16]{3,0,4,2,1:T(8,128)} %fusion.8, ...), kind=kOutput, calls=%fused_computation.12 | convolution fusion | flops 158862848 | bytes 18876416 | tf_op jit(solution)/shard_map/...ab,ac->...cb/dot_general | solution.py:32
  278.6 22.6 %fusion.30 = f32[16,12,8,32,16]{3,0,4,2,1:T(8,128)} fusion(f32[12,8,32,16,16]{2,3,4,1,0:T(8,128)} %get-tuple-element.8), kind=kOutput, calls=%fused_computation.41 | convolution fusion | flops 150998528 | bytes 6291456 | tf_op jit(solution)/shard_map/...cb,bd->...dc/dot_general | solution.py:42
  301.1 14.4 %fusion.28 = f32[16,12,8,32,16]{3,0,4,2,1:T(8,128)} fusion(f32[12,8,32,16,16]{2,3,4,1,0:T(8,128)S(1)} %copy-done.2), kind=kOutput, calls=%fused_computation.39 | convolution fusion | flops 150998528 | bytes 6291456 | tf_op jit(solution)/shard_map/...cb,bd->...dc/dot_general | solution.py:42
  315.5 23.7 %add_bitcast_fusion.2 = f32[12,8,32,16,16]{2,3,4,1,0:T(8,128)} fusion(f32[16,12,8,32,16]{3,0,4,2,1:T(8,128)} %fusion.28, f32[12,8,32,16,16]{2,3,4,1,0:T(8,128)} %get-tuple-element.7), kind=kOutput, calls=%fused_computation.9 | convolution fusion | flops 152571392 | bytes 9437184 | tf_op jit(solution)/shard_map/...cb,bd->...dc/dot_general | solution.py:42
  339.2 15.2 %copy.198 = f32[12,8,32,16,16]{2,4,3,1,0:T(8,128)} copy(f32[12,8,32,16,16]{2,3,4,1,0:T(8,128)} %add_bitcast_fusion.2) | data formatting | bytes 6291456 | tf_op jit(solution)/shard_map/add | solution.py:45
  377.4 23.5 %subtract_bitcast_fusion.2 = f32[12,8,32,16,16]{2,3,4,1,0:T(8,128)} fusion(f32[16,12,8,32,16]{3,0,4,2,1:T(8,128)} %fusion.30, f32[12,8,32,16,16]{2,3,4,1,0:T(8,128)} %get-tuple-element.7), kind=kOutput, calls=%fused_computation.10 | convolution fusion | flops 152571392 | bytes 9437184 | tf_op jit(solution)/shard_map/...cb,bd->...dc/dot_general | solution.py:42
  400.8 15.2 %copy.193 = f32[12,8,32,16,16]{2,4,3,1,0:T(8,128)} copy(f32[12,8,32,16,16]{2,3,4,1,0:T(8,128)} %subtract_bitcast_fusion.2) | data formatting | bytes 6291456 | tf_op jit(solution)/shard_map/sub | solution.py:44
  503.9 25.3 %fusion.57 = f32[2,12,8,32,256]{4,1,3,2,0:T(8,128)} fusion(f32[2,12,8,32,256]{4,1,3,2,0:T(8,128)} %pad_maximum_fusion, f32[3,8,32,256]{3,0,2,1:T(4,128)S(1)} %copy-done.21, f32[3,12,12]{2,1,0:T(8,128)S(1)} %copy-done.26), kind=kOutput, calls=%fused_computation.67 | convolution fusion | flops 684195840 | bytes 13371072 | tf_op jit(solution)/shard_map/mab,mcb...->ca.../dot_general | solution.py:71
  530.8 12.1 %fusion.54 = (f32[12,8,32,256]{3,0,2,1:T(8,128)}, f32[12,8,32,256]{3,0,2,1:T(8,128)}) fusion(f32[12,8,32,256]{3,0,2,1:T(8,128)} %bitcast.351, f32[2,12,8,32,256]{4,1,3,2,0:T(8,128)} %fusion.57, f32[12,32,256]{2,0,1:T(8,128)} %get-tuple-element.19, pred[8]{0:T(512)(128)(4,1)S(1)} %copy-done.38, f32[12,8,32,256]{3,0,2,1:T(8,128)} %bitcast.356, ...), kind=kLoop, calls=%fused_computation.64 | loop fusion | flops 3145728 | bytes 19660808 | tf_op jit(solution)/shard_map/jit(_where)/select_n | solution.py:128
  551.8 22.3 %fusion.20 = f32[16,12,8,32,16]{3,0,4,2,1:T(8,128)} fusion(f32[12,8,32,16,16]{2,4,3,1,0:T(8,128)} %bitcast.331), kind=kOutput, calls=%fused_computation.31 | convolution fusion | flops 150998528 | bytes 6291456 | tf_op jit(solution)/shard_map/...ab,ac->...cb/dot_general | solution.py:32
  574.1 14.6 %fusion.22 = f32[16,12,8,32,16]{3,0,4,2,1:T(8,128)} fusion(f32[12,8,32,16,16]{2,4,3,1,0:T(8,128)S(1)} %bitcast.332), kind=kOutput, calls=%fused_computation.33 | convolution fusion | flops 150998528 | bytes 6291456 | tf_op jit(solution)/shard_map/...ab,ac->...cb/dot_general | solution.py:32
  597.6 20.8 %fusion.24 = f32[16,12,8,32,16]{3,0,4,2,1:T(8,128)} fusion(f32[12,8,32,16,16]{2,4,3,1,0:T(8,128)} %bitcast.329), kind=kOutput, calls=%fused_computation.35 | convolution fusion | flops 150998528 | bytes 6291456 | tf_op jit(solution)/shard_map/...ab,ac->...cb/dot_general | solution.py:32
  618.3 33.8 %subtract_bitcast_fusion.1 = (f32[12,8,32,16,16]{2,3,4,1,0:T(8,128)}, f32[12,8,32,16,16]{2,3,4,1,0:T(8,128)}) fusion(f32[16,16]{0,1:T(8,128)S(1)} %copy-done.29, f32[16,16]{0,1:T(8,128)S(1)} %copy-done.28, f32[16,12,8,32,16]{3,0,4,2,1:T(8,128)} %fusion.20, f32[16,12,8,32,16]{3,0,4,2,1:T(8,128)} %fusion.24, f32[16,12,8,32,16]{3,0,4,2,1:T(8,128)} %fusion.22, ...), kind=kOutput, calls=%fused_computation.6 | convolution fusion | flops 157289984 | bytes 18876416 | tf_op jit(solution)/shard_map/...ab,ac->...cb/dot_general | solution.py:32
  652.1 22.4 %fusion.14 = f32[16,12,8,32,16]{3,0,4,2,1:T(8,128)} fusion(f32[12,8,32,16,16]{2,3,4,1,0:T(8,128)} %get-tuple-element.6), kind=kOutput, calls=%fused_computation.25 | convolution fusion | flops 150998528 | bytes 6291456 | tf_op jit(solution)/shard_map/...cb,bd->...dc/dot_general | solution.py:42
  674.5 14.7 %fusion.12 = f32[16,12,8,32,16]{3,0,4,2,1:T(8,128)} fusion(f32[12,8,32,16,16]{2,3,4,1,0:T(8,128)S(1)} %copy-done.1), kind=kOutput, calls=%fused_computation.23 | convolution fusion | flops 150998528 | bytes 6291456 | tf_op jit(solution)/shard_map/...cb,bd->...dc/dot_general | solution.py:42
  689.2 23.0 %add_bitcast_fusion = f32[12,8,32,16,16]{2,3,4,1,0:T(8,128)} fusion(f32[16,12,8,32,16]{3,0,4,2,1:T(8,128)} %fusion.12, f32[12,8,32,16,16]{2,3,4,1,0:T(8,128)} %get-tuple-element.5), kind=kOutput, calls=%fused_computation.3 | convolution fusion | flops 151784960 | bytes 9437184 | tf_op jit(solution)/shard_map/...cb,bd->...dc/dot_general | solution.py:42
  712.2 15.2 %copy.232 = f32[12,8,32,16,16]{2,4,3,1,0:T(8,128)} copy(f32[12,8,32,16,16]{2,3,4,1,0:T(8,128)} %add_bitcast_fusion) | data formatting | bytes 6291456 | tf_op jit(solution)/shard_map/add | solution.py:45
  750.3 23.0 %subtract_bitcast_fusion = f32[12,8,32,16,16]{2,3,4,1,0:T(8,128)} fusion(f32[16,12,8,32,16]{3,0,4,2,1:T(8,128)} %fusion.14, f32[12,8,32,16,16]{2,3,4,1,0:T(8,128)} %get-tuple-element.5), kind=kOutput, calls=%fused_computation.4 | convolution fusion | flops 151784960 | bytes 9437184 | tf_op jit(solution)/shard_map/...cb,bd->...dc/dot_general | solution.py:42
  773.3 15.2 %copy.227 = f32[12,8,32,16,16]{2,4,3,1,0:T(8,128)} copy(f32[12,8,32,16,16]{2,3,4,1,0:T(8,128)} %subtract_bitcast_fusion) | data formatting | bytes 6291456 | tf_op jit(solution)/shard_map/sub | solution.py:44
  824.5 11.4 %copy.240 = f32[12,8,32,256]{2,1,0,3:T(8,128)} copy(f32[12,8,32,256]{3,2,1,0:T(8,128)} %bitcast.371) | data formatting | bytes 6291456 | tf_op jit(solution)/shard_map/transpose | solution.py:53
  835.9 14.1 %reshape.543 = f32[16,1,49152]{2,1,0:T(1,128)} reshape(f32[256,12,8,32]{3,2,1,0:T(8,128)} %bitcast.347) | data formatting | bytes 6291456
  873.1 11.4 %copy.247 = f32[12,8,32,256]{2,1,0,3:T(8,128)} copy(f32[12,8,32,256]{3,2,1,0:T(8,128)} %bitcast.372) | data formatting | bytes 6291456 | tf_op jit(solution)/shard_map/transpose | solution.py:53
  884.5 14.1 %reshape.541 = f32[16,1,49152]{2,1,0:T(1,128)} reshape(f32[256,12,8,32]{3,2,1,0:T(8,128)} %bitcast.348) | data formatting | bytes 6291456
  898.6 17.2 %all-to-all-done.2 = f32[16,1,49152]{2,1,0:T(1,128)} async-done(((f32[16,1,49152]{2,1,0:T(1,128)}), f32[16,1,49152]{2,1,0:T(1,128)}, u32[]{:S(2)}, u32[]{:S(2)}) %all-to-all-start.2) | async-done | bytes 3145760 | tf_op jit(solution)/shard_map/all_to_all | solution.py:138
  915.8 15.9 %all-to-all-start.3 = ((f32[16,1,49152]{2,1,0:T(1,128)}), f32[16,1,49152]{2,1,0:T(1,128)}, u32[]{:S(2)}, u32[]{:S(2)}) async-start(f32[16,1,49152]{2,1,0:T(1,128)} %reshape.541), calls=%async_computation.3 | async-start | bytes 6291456 | tf_op jit(solution)/shard_map/all_to_all | solution.py:141
  939.6 11.8 %reduce.3 = f32[16,49152]{1,0:T(8,128)} reduce(f32[16,1,49152]{2,1,0:T(1,128)} %all-to-all-done.2, f32[]{:T(128)} %broadcast.918), dimensions={1}, to_apply=%all_to_all.60.reduce_sub_computation | reduce | bytes 6291460 | tf_op jit(solution)/shard_map/all_to_all | solution.py:138
  951.4 12.3 %reshape.544 = f32[256,12,8,32]{3,2,1,0:T(8,128)} reshape(f32[16,49152]{1,0:T(8,128)} %reduce.3) | data formatting | bytes 6291456
  963.8 16.4 %copy.242 = f32[12,16,8,32,16]{3,4,2,1,0:T(8,128)} copy(f32[12,16,8,32,16]{3,2,0,4,1:T(8,128)} %bitcast.341) | data formatting | bytes 6291456 | tf_op jit(solution)/shard_map/all_to_all | solution.py:138
  991.1 11.8 %reduce.2 = f32[16,49152]{1,0:T(8,128)} reduce(f32[16,1,49152]{2,1,0:T(1,128)} %all-to-all-done.3, f32[]{:T(128)} %broadcast.918), dimensions={1}, to_apply=%all_to_all.64.reduce_sub_computation | reduce | bytes 6291460 | tf_op jit(solution)/shard_map/all_to_all | solution.py:141
  1002.9 12.4 %reshape.542 = f32[256,12,8,32]{3,2,1,0:T(8,128)} reshape(f32[16,49152]{1,0:T(8,128)} %reduce.2) | data formatting | bytes 6291456
  1015.4 16.4 %copy.249 = f32[12,16,8,32,16]{3,4,2,1,0:T(8,128)} copy(f32[12,16,8,32,16]{3,2,0,4,1:T(8,128)} %bitcast.343) | data formatting | bytes 6291456 | tf_op jit(solution)/shard_map/all_to_all | solution.py:141
  1041.0 17.7 %multiply_reduce_fusion = (f32[]{:T(128)}, f32[12,16,32,256]{3,2,1,0:T(8,128)}, f32[12,16,32,256]{3,2,1,0:T(8,128)}) fusion(f32[12,16,32,256]{3,2,1,0:T(8,128)} %param.7, f32[16,32,256]{2,1,0:T(8,128)} %param.9, f32[12]{0:T(128)S(1)} %convert_element_type.195, f32[12,16,32,256]{3,0,2,1:T(8,128)} %fusion.55, f32[128,256]{1,0:T(8,128)S(1)} %get-tuple-element.29, ...), kind=kOutput, calls=%fused_computation.58 | convolution fusion | flops 4850843648 | bytes 32243764 | tf_op jit(solution)/shard_map/dot_general | solution.py:146
  1058.8 44.0 %psum.7 = f32[]{:T(128)} all-reduce(f32[]{:T(128)} %get-tuple-element.3), channel_id=1, replica_groups=mesh['sys'=2,'slab'=16] {'slab'}, use_global_device_ids=true, to_apply=%region_1.2 | all-reduce | flops 1 | bytes 8 | tf_op jit(solution)/shard_map/psum | solution.py:154
  (163 shorter events, 259.8 us)
Async XLA Ops:
  0.6 931.7 %copy-start = (f32[6,16,32,256]{3,2,1,0:T(8,128)S(1)}, f32[6,16,32,256]{3,2,1,0:T(8,128)}, u32[]{:S(2)}) copy-start(f32[6,16,32,256]{3,2,1,0:T(8,128)} %param.8) | copy-start | bytes 9437188
  0.7 0.6 copy-start.33
  0.7 0.6 copy-start.35
  42.1 67.1 %all-to-all-start.1 = ((f32[16,1,49152]{2,1,0:T(1,128)}), f32[16,1,49152]{2,1,0:T(1,128)}, u32[]{:S(2)}, u32[]{:S(2)}) async-start(f32[16,1,49152]{2,1,0:T(1,128)} %reshape.539), calls=%async_computation.1 | async-start | bytes 6291456 | tf_op jit(solution)/shard_map/all_to_all | solution.py:104
  90.3 34.8 %copy-start.39 = (f32[3]{0:T(128)S(1)}, f32[3]{0:T(128)}, u32[]{:S(2)}) copy-start(f32[3]{0:T(128)} %param.13) | copy-start | bytes 40
  109.2 87.0 %all-to-all-start = ((f32[16,1,49152]{2,1,0:T(1,128)}), f32[16,1,49152]{2,1,0:T(1,128)}, u32[]{:S(2)}, u32[]{:S(2)}) async-start(f32[16,1,49152]{2,1,0:T(1,128)} %reshape.537), calls=%async_computation | async-start | bytes 6291456 | tf_op jit(solution)/shard_map/all_to_all | solution.py:103
  126.4 306.3 %copy-start.30 = (f32[8,4]{0,1:T(4,128)}, f32[8,4]{0,1:T(4,128)S(1)}, u32[]{:S(2)}) copy-start(f32[8,4]{0,1:T(4,128)S(1)} %get-tuple-element.36) | copy-start | bytes 388
  127.1 117.9 %copy-start.27 = (f32[16,16]{0,1:T(8,128)}, f32[16,16]{0,1:T(8,128)S(1)}, u32[]{:S(2)}) copy-start(f32[16,16]{0,1:T(8,128)S(1)} %get-tuple-element.34) | copy-start | bytes 3076
  154.1 24.5 %copy-start.4 = (f32[128,12,16,32]{3,2,1,0:T(8,128)S(1)}, f32[128,12,16,32]{3,2,1,0:T(8,128)}, u32[]{:S(2)}) copy-start(f32[128,12,16,32]{3,2,1,0:T(8,128)} %reshape.540) | copy-start | bytes 9437188
  278.6 22.6 %copy-start.2 = (f32[12,8,32,16,16]{2,3,4,1,0:T(8,128)S(1)}, f32[12,8,32,16,16]{2,3,4,1,0:T(8,128)}, u32[]{:S(2)}) copy-start(f32[12,8,32,16,16]{2,3,4,1,0:T(8,128)} %get-tuple-element.8) | copy-start | bytes 9437188
  363.5 8.0 copy-start.15
  425.3 7.4 copy-start.17
  425.3 7.4 copy-start.19
  437.8 6.0 copy-start.9
  437.8 12.4 %copy-start.11 = (f32[12,8,256,8,4]{2,3,4,1,0:T(8,128)}, f32[12,8,256,8,4]{2,3,4,1,0:T(8,128)S(1)}, u32[]{:S(2)}) copy-start(f32[12,8,256,8,4]{2,3,4,1,0:T(8,128)S(1)} %get-tuple-element.13) | copy-start | bytes 9437188
  452.1 2.0 copy-start.7
  457.0 11.4 %copy-start.12 = (f32[12,8,256,8,4]{2,3,4,1,0:T(8,128)S(1)}, f32[12,8,256,8,4]{2,3,4,1,0:T(8,128)}, u32[]{:S(2)}) copy-start(f32[12,8,256,8,4]{2,3,4,1,0:T(8,128)} %copy-done.11) | copy-start | bytes 9437188
  476.9 2.0 copy-start.5
  491.3 3.2 copy-start.25
  491.3 3.2 copy-start.26
  494.3 5.2 copy-start.6
  494.3 5.2 copy-start.8
  499.6 4.3 copy-start.21
  503.9 25.3 %copy-start.22 = (f32[12,1,32,255]{3,0,2,1:T(8,128)S(1)}, f32[12,1,32,255]{3,0,2,1:T(8,128)}, u32[]{:S(2)}) copy-start(f32[12,1,32,255]{3,0,2,1:T(8,128)} %get-tuple-element.23) | copy-start | bytes 1175044
  503.9 25.3 %copy-start.23 = (f32[12,1,32,255]{3,0,2,1:T(8,128)S(1)}, f32[12,1,32,255]{3,0,2,1:T(8,128)}, u32[]{:S(2)}) copy-start(f32[12,1,32,255]{3,0,2,1:T(8,128)} %get-tuple-element.21) | copy-start | bytes 1175044
  503.9 25.3 %copy-start.24 = (f32[12,1,32,1]{3,0,2,1:T(8,128)S(1)}, f32[12,1,32,1]{3,0,2,1:T(8,128)}, u32[]{:S(2)}) copy-start(f32[12,1,32,1]{3,0,2,1:T(8,128)} %copy.208) | copy-start | bytes 4612
  529.2 1.6 copy-start.38
  551.8 22.3 %copy-start.3 = (f32[12,8,32,256]{2,3,1,0:T(8,128)S(1)}, f32[12,8,32,256]{2,3,1,0:T(8,128)}, u32[]{:S(2)}) copy-start(f32[12,8,32,256]{2,3,1,0:T(8,128)} %copy.221) | copy-start | bytes 9437188
  597.6 20.8 %copy-start.28 = (f32[16,16]{0,1:T(8,128)S(1)}, f32[16,16]{0,1:T(8,128)}, u32[]{:S(2)}) copy-start(f32[16,16]{0,1:T(8,128)} %copy-done.27) | copy-start | bytes 3076
  597.6 20.8 %copy-start.29 = (f32[16,16]{0,1:T(8,128)S(1)}, f32[16,16]{0,1:T(8,128)}, u32[]{:S(2)}) copy-start(f32[16,16]{0,1:T(8,128)} %fusion.207) | copy-start | bytes 3076
  652.1 22.4 %copy-start.1 = (f32[12,8,32,16,16]{2,3,4,1,0:T(8,128)S(1)}, f32[12,8,32,16,16]{2,3,4,1,0:T(8,128)}, u32[]{:S(2)}) copy-start(f32[12,8,32,16,16]{2,3,4,1,0:T(8,128)} %get-tuple-element.6) | copy-start | bytes 9437188
  736.4 8.0 copy-start.16
  797.7 7.3 copy-start.18
  797.7 7.3 copy-start.20
  797.7 7.3 copy-start.31
  797.7 7.3 copy-start.32
  809.9 12.2 %copy-start.10 = (f32[12,8,256,8,4]{2,3,4,1,0:T(8,128)}, f32[12,8,256,8,4]{2,3,4,1,0:T(8,128)S(1)}, u32[]{:S(2)}) copy-start(f32[12,8,256,8,4]{2,3,4,1,0:T(8,128)S(1)} %get-tuple-element.12) | copy-start | bytes 9437188
  810.0 12.1 %copy-start.13 = (f32[12,8,256,8,4]{2,3,4,1,0:T(8,128)}, f32[12,8,256,8,4]{2,3,4,1,0:T(8,128)S(1)}, u32[]{:S(2)}) copy-start(f32[12,8,256,8,4]{2,3,4,1,0:T(8,128)S(1)} %get-tuple-element.11) | copy-start | bytes 9437188
  850.0 65.8 %all-to-all-start.2 = ((f32[16,1,49152]{2,1,0:T(1,128)}), f32[16,1,49152]{2,1,0:T(1,128)}, u32[]{:S(2)}, u32[]{:S(2)}) async-start(f32[16,1,49152]{2,1,0:T(1,128)} %reshape.543), calls=%async_computation.2 | async-start | bytes 6291456 | tf_op jit(solution)/shard_map/all_to_all | solution.py:138
  856.4 8.1 copy-start.14
  898.6 33.1 %copy-start.40 = (s32[12]{0:T(128)S(1)}, s32[12]{0:T(128)}, u32[]{:S(2)}) copy-start(s32[12]{0:T(128)} %param.11) | copy-start | bytes 148
  898.6 33.1 %copy-start.34 = (f32[256]{0:T(256)S(1)}, f32[256]{0:T(256)}, u32[]{:S(2)}) copy-start(f32[256]{0:T(256)} %copy-done.33) | copy-start | bytes 3076
  898.6 33.1 %copy-start.36 = (pred[128]{0:T(512)(128)(4,1)S(1)}, pred[128]{0:T(512)(128)(4,1)}, u32[]{:S(2)}) copy-start(pred[128]{0:T(512)(128)(4,1)} %copy-done.35) | copy-start | bytes 388
  898.6 33.7 %copy-start.37 = (s32[12]{0:T(128)S(1)}, s32[12]{0:T(128)}, u32[]{:S(2)}) copy-start(s32[12]{0:T(128)} %param.10) | copy-start | bytes 148
  915.8 75.3 %all-to-all-start.3 = ((f32[16,1,49152]{2,1,0:T(1,128)}), f32[16,1,49152]{2,1,0:T(1,128)}, u32[]{:S(2)}, u32[]{:S(2)}) async-start(f32[16,1,49152]{2,1,0:T(1,128)} %reshape.541), calls=%async_computation.3 | async-start | bytes 6291456 | tf_op jit(solution)/shard_map/all_to_all | solution.py:141
where the time goes:
time: 1110 us
  matrix products  543 us (49%)
  local copies, waits for them, and re-layouts  350 us (32%)
  other arithmetic  80.6 us (7%)
  starting transfers between devices  45.8 us (4%)
  blocking collectives  44 us (4%)
  waiting for transfers between devices  37.5 us (3%)
    dot_general x16, matrix products, outer_apply(): return jnp.einsum('...ab,ac->...cb', values, factors, precision=precise)  244 us
    dot_general x16, matrix products, inner_apply(): return jnp.einsum('...cb,bd->...dc', values, factors, precision=precise)  221 us
    unnamed x90, local copies, waits for them, and re-layouts  111 us
    psum x1, blocking collectives, body(): summed_sq = lax.psum(jnp.sum(change * change), 'slab')  44 us
    add x3, local copies, waits for them, and re-layouts, dft_last(): inner_apply(turned_imag, inner_cos)  32.8 us
    sub x3, local copies, waits for them, and re-layouts, dft_last(): inner_apply(turned_real, inner_cos)  32.7 us
    dot_general x3, matrix products, mix_sites(): mixed = jnp.einsum('mab,mcb...->ca...', chi_amp, scaled, precision=precise)  30.3 us
    all_to_all x2, local copies, waits for them, and re-layouts, body(): lax.all_to_all(back_real, 'slab', split_axis=3, concat_axis=1, tiled=True)  25.9 us
  transfers between devices with their start and end apart: 4, of which 3 were waited for; matrix products, arithmetic and copies ran while one was open for 19% of the time, Pallas kernels for 0%

commit v1 on v0

v1 whole, which is shorter than its diff:
```python
import math

import jax
import jax.numpy as jnp
import ml_dtypes
import numpy as np
from jax import lax
from jax.experimental import pallas as pl
from jax.experimental.pallas import tpu as pltpu
from jax.sharding import PartitionSpec as P

full_turn = 2.0 * math.pi
precise = lax.Precision.HIGHEST
f32 = jnp.float32
bf16 = jnp.bfloat16


def hartley(n):
    product = np.outer(np.arange(n), np.arange(n)) % n
    theta = product * (full_turn / n)
    return (np.cos(theta) + np.sin(theta)) / math.sqrt(n)


def halves(matrix):
    high = matrix.astype(ml_dtypes.bfloat16)
    low = (matrix - high.astype(np.float64)).astype(ml_dtypes.bfloat16)
    return jnp.asarray(np.stack((high, low)))


def signed_square(n):
    index = np.arange(n)
    freq = ((index + n // 2) % n - n // 2) / n
    return (full_turn * full_turn * freq * freq).astype(np.float32)


def split(values):
    high = values.astype(bf16)
    return high, (values - high.astype(f32)).astype(bf16)


def mul(left, right):
    return jnp.dot(left, right, preferred_element_type=f32)


def left_by(table, values):
    high, low = split(values)
    return mul(table[0], high) + (mul(table[0], low) + mul(table[1], high))


def right_by(values, table):
    high, low = split(values)
    return mul(high, table[0]) + (mul(low, table[0]) + mul(high, table[1]))


def head_kernel(x_ref, b_ref, z_ref, *outs):
    rows, depth, columns = x_ref.shape[1:]
    devices = outs[0].shape[0]
    group = z_ref.shape[1] // depth
    for i in range(rows // group):
        part = x_ref[0, i * group:(i + 1) * group].reshape(group * depth, columns)
        turned = left_by(z_ref, right_by(part, b_ref)).reshape(depth, group, columns)
        for j, out in enumerate(outs):
            out[:, 0, i * group:(i + 1) * group, :] = turned[j * devices:(j + 1) * devices]


def middle_kernel(amp_ref, width_ref, kz_ref, x_ref, a_ref, ka_ref, kb_ref, out_ref, work_ref):
    devices, sites, rows, columns = x_ref.shape
    terms = width_ref.shape[0]
    extent = devices * rows
    for s in range(sites):
        work_ref[s] = left_by(a_ref, x_ref[:, s].reshape(extent, columns))

    @pl.loop(0, extent // 8)
    def _(step):
        here = pl.ds(pl.multiple_of(step * 8, 8), 8)
        square = ka_ref[here, :] + kb_ref[...] + kz_ref[0]
        weights = [jnp.exp(-width_ref[m] * square) for m in range(terms)]
        values = [work_ref[t, here, :] for t in range(sites)]
        for s in range(sites):
            total = values[s]
            for t in range(sites):
                factor = amp_ref[s * sites + t] * weights[0]
                for m in range(1, terms):
                    factor = factor + amp_ref[(m * sites + s) * sites + t] * weights[m]
                total = total + factor * values[t]
            work_ref[s, here, :] = total

    for s in range(sites):
        out_ref[:, s] = left_by(a_ref, work_ref[s]).reshape(devices, rows, columns)


def tail_kernel(species_ref, charge_ref, *refs):
    count = len(refs) - 8
    parts = refs[:count]
    x_ref, lj_ref, pot_ref, b_ref, z_ref, total_ref, next_ref, sum_ref = refs[count:]
    site = pl.program_id(0)
    rows, depth, columns = x_ref.shape[1:]
    devices = parts[0].shape[0]
    group = z_ref.shape[1] // depth

    @pl.when(site == 0)
    def _():
        sum_ref[...] = jnp.zeros_like(sum_ref)

    charge = charge_ref[site]
    for i in range(rows // group):
        here = slice(i * group, (i + 1) * group)
        blocks = [part[:, 0, here, :].reshape(devices * group, columns) for part in parts]
        joined = jnp.concatenate(blocks, axis=0) if count > 1 else blocks[0]
        total = right_by(left_by(z_ref, joined), b_ref).reshape(group, depth, columns)
        before = x_ref[0, here]
        indirect = total - before
        shifted = indirect - (lj_ref[0, here] + charge * pot_ref[here])
        after = jnp.where(shifted < 0, jnp.exp(jnp.minimum(shifted, 0.0)) - 1.0, shifted) - indirect
        change = after - before
        total_ref[0, here] = total
        next_ref[0, here] = after
        sum_ref[...] += jnp.sum((change * change).reshape(-1, 8, columns), axis=0)


def plain_mix(values, square, chi_amp, chi_width):
    weight = jnp.exp(-chi_width.reshape((-1,) + (1,) * square.ndim) * square[None])
    scaled = weight[:, None] * values[None]
    return values + jnp.einsum("mab,mb...->a...", chi_amp, scaled, precision=precise)


def convolved_plain(x, chi_amp, chi_width, me, devices):
    sites, rows, depth, columns = x.shape
    extent = rows * devices
    b_table = jnp.asarray(hartley(columns), f32)
    z_table = jnp.asarray(hartley(depth), f32)
    a_table = jnp.asarray(hartley(extent), f32)
    y = jnp.einsum("sazb,bk->sazk", x, b_table, precision=precise)
    y = jnp.einsum("sazk,zl->salk", y, z_table, precision=precise)
    share = depth * columns // devices
    y = y.reshape(sites, rows, devices, share).transpose(2, 0, 1, 3)
    y = lax.all_to_all(y, "slab", split_axis=0, concat_axis=0)
    y = jnp.einsum("dsrc,drk->skc", y, a_table.reshape(devices, rows, extent), precision=precise)
    plane = (signed_square(depth)[:, None] + signed_square(columns)[None, :]).reshape(devices, share)
    mine = lax.dynamic_index_in_dim(jnp.asarray(plane), me, 0, keepdims=False)
    square = jnp.asarray(signed_square(extent))[:, None] + mine[None, :]
    y = plain_mix(y, square, chi_amp, chi_width)
    y = jnp.einsum("skc,drk->dsrc", y, a_table.reshape(devices, rows, extent), precision=precise)
    y = lax.all_to_all(y, "slab", split_axis=0, concat_axis=0)
    y = y.transpose(1, 2, 0, 3).reshape(sites, rows, depth, columns)
    y = jnp.einsum("salk,zl->sazk", y, z_table, precision=precise)
    return jnp.einsum("sazk,bk->sazb", y, b_table, precision=precise)


def closure_plain(total_corr, correlation, lj_field, potential, species, charges):
    indirect = total_corr - correlation
    energy = lj_field[species] + charges.astype(f32)[:, None, None, None] * potential[None]
    shifted = indirect - energy
    next_corr = jnp.where(shifted < 0, jnp.expm1(jnp.minimum(shifted, 0.0)), shifted) - indirect
    change = next_corr - correlation
    return next_corr, change * change


vmem = pl.BlockSpec(memory_space=pltpu.VMEM)
smem = pl.BlockSpec(memory_space=pltpu.SMEM)
limit = 56 * 1024 * 1024


def body(correlation, lj_field, potential, species, charges, chi_amp, chi_width):
    sites, rows, depth, columns = correlation.shape
    devices = lax.axis_size("slab")
    me = lax.axis_index("slab")
    extent = rows * devices
    cells = sites * extent * depth * columns

    if depth % devices or rows % 8 or columns % 128:
        total_corr = convolved_plain(correlation, chi_amp, chi_width, me, devices)
        next_corr, squares = closure_plain(
            total_corr, correlation, lj_field, potential, species, charges
        )
        summed = lax.psum(jnp.sum(squares), "slab")
        return (total_corr, next_corr, jnp.sqrt(summed / cells + 1e-06).reshape(1))

    group = 8
    chunks = depth // devices
    z_basis = hartley(depth)
    forward = np.einsum("kz,ab->kabz", z_basis, np.eye(group)).reshape(group * depth, group * depth)
    b_table = halves(hartley(columns))
    a_table = halves(hartley(extent))
    z_table = halves(forward)
    z_back = halves(forward.T)
    b_spec = pl.BlockSpec((2, columns, columns), lambda s, *_: (0, 0, 0))
    z_spec = pl.BlockSpec((2, group * depth, group * depth), lambda s, *_: (0, 0, 0))
    row_spec = pl.BlockSpec((1, rows, depth, columns), lambda s, *_: (s, 0, 0, 0))
    part_spec = pl.BlockSpec((devices, 1, rows, columns), lambda s, *_: (0, s, 0, 0))
    part_shape = jax.ShapeDtypeStruct((devices, sites, rows, columns), f32)
    size = correlation.size

    sent = pl.pallas_call(
        head_kernel,
        grid=(sites,),
        in_specs=[row_spec, b_spec, z_spec],
        out_specs=[part_spec] * chunks,
        out_shape=[part_shape] * chunks,
        compiler_params=pltpu.CompilerParams(vmem_limit_bytes=limit),
        cost_estimate=pl.CostEstimate(
            flops=12 * size * columns, bytes_accessed=8 * size, transcendentals=0
        ),
        name="head",
    )(correlation, b_table, z_table)

    kz = jnp.asarray(signed_square(depth))
    ka = jnp.asarray(np.repeat(signed_square(extent)[:, None], columns, axis=1))
    kb = jnp.asarray(np.repeat(signed_square(columns)[None, :], 8, axis=0))
    amp = chi_amp.reshape(-1)
    arrived = []
    for j in range(chunks):
        got = lax.all_to_all(sent[j], "slab", split_axis=0, concat_axis=0, tiled=True)
        mixed = pl.pallas_call(
            middle_kernel,
            in_specs=[smem, smem, smem, vmem, vmem, vmem, vmem],
            out_specs=vmem,
            out_shape=part_shape,
            scratch_shapes=[pltpu.VMEM((sites, extent, columns), f32)],
            compiler_params=pltpu.CompilerParams(vmem_limit_bytes=limit),
            cost_estimate=pl.CostEstimate(
                flops=20 * size * extent // chunks, bytes_accessed=8 * size // chunks, transcendentals=0
            ),
            name="middle",
        )(amp, chi_width, lax.dynamic_slice(kz, (j * devices + me,), (1,)), got, a_table, ka, kb)
        arrived.append(lax.all_to_all(mixed, "slab", split_axis=0, concat_axis=0, tiled=True))

    total_corr, next_corr, sums = pl.pallas_call(
        tail_kernel,
        grid_spec=pltpu.PrefetchScalarGridSpec(
            num_scalar_prefetch=2,
            grid=(sites,),
            in_specs=[part_spec] * chunks + [
                row_spec,
                pl.BlockSpec((1, rows, depth, columns), lambda s, kind, _: (kind[s], 0, 0, 0)),
                pl.BlockSpec((rows, depth, columns), lambda s, *_: (0, 0, 0)),
                b_spec,
                z_spec,
            ],
            out_specs=[row_spec, row_spec, pl.BlockSpec((8, columns), lambda s, *_: (0, 0))],
        ),
        out_shape=[
            jax.ShapeDtypeStruct(correlation.shape, f32),
            jax.ShapeDtypeStruct(correlation.shape, f32),
            jax.ShapeDtypeStruct((8, columns), f32),
        ],
        compiler_params=pltpu.CompilerParams(vmem_limit_bytes=limit),
        cost_estimate=pl.CostEstimate(
            flops=12 * size * columns, bytes_accessed=20 * size, transcendentals=size
        ),
        name="tail",
    )(species, charges.astype(f32), *arrived, correlation, lj_field, potential, b_table, z_back)
    summed = lax.psum(jnp.sum(sums), "slab")
    return (total_corr, next_corr, jnp.sqrt(summed / cells + 1e-06).reshape(1))


def solution(mesh):
    placed = (
        P("sys", "slab", None, None),
        P("sys", "slab", None, None),
        P(("sys", "slab"), None, None),
        P(),
        P(),
        P(),
        P(),
    )
    return jax.shard_map(
        body,
        mesh=mesh,
        in_specs=placed,
        out_specs=(P("sys", "slab", None, None), P("sys", "slab", None, None), P("sys")),
        check_vma=False,
    )
```

time: 1110 us -> 377 us (0.34)
  matrix products: 543 us -> 0 us
  local copies, waits for them, and re-layouts: 350 us -> 4.67 us
  waiting for transfers between devices: 37.5 us -> 139 us
  other arithmetic: 80.6 us -> 1.81 us
  blocking collectives: 44 us -> 121 us
  Pallas kernels: 0 us -> 70.3 us
    dot_general x39 -> x0, matrix products: 543 us -> none  [the longest x16 244 us: outer_apply(): return jnp.einsum('...ab,ac->...cb', values, factors, precision=precise)]
    unnamed x90 -> x10, local copies, waits for them, and re-layouts: 111 us -> 3.37 us
    all_to_all x4 -> x3, waiting for transfers between devices: 37.5 us -> 139 us  [the longest x2 99.7 us: body(): lax.all_to_all(mixed, 'slab', split_axis=0, concat_axis=0, tiled=True)]
    all_to_all x0 -> x1, blocking collectives: none -> 77.3 us  [body(): lax.all_to_all(sent[j], 'slab', split_axis=0, concat_axis=0, tiled=True)]
    pallas_call x0 -> x4, Pallas kernels: none -> 70.3 us  [the longest x2 37.1 us: body(): pl.pallas_call(middle_kernel, in_specs=[smem, smem, smem, vmem, vmem, vme...]
    transpose x6 -> x0, local copies, waits for them, and re-layouts: 59.4 us -> none  [the longest x2 22.8 us: dft_along(): return (jnp.moveaxis(out_real, -1, axis), jnp.moveaxis(out_imag, -1, axis))]
    all_to_all x5 -> x0, local copies, waits for them, and re-layouts: 52.1 us -> none  [the longest x2 25.9 us: body(): lax.all_to_all(back_real, 'slab', split_axis=3, concat_axis=1, tiled=True)]
    all_to_all x4 -> x0, other arithmetic: 47.3 us -> none  [the longest x1 11.8 us: body(): lax.all_to_all(spec_real, 'slab', split_axis=3, concat_axis=1, tiled=True)]
  transfers between devices with their start and end apart: 4 -> 3, of which waited for: 3 -> 3; matrix products, arithmetic and copies ran while one was open for 19% -> 0% of each run, Pallas kernels for 0% -> 10%
where the time goes in v1:
time: 377 us; the launch traced here: 376 us
  waiting for transfers between devices  139 us (37%)
  blocking collectives  121 us (32%)
  Pallas kernels  70.3 us (19%)
  starting transfers between devices  36.2 us (10%)
  local copies, waits for them, and re-layouts  4.67 us (1%)
    all_to_all x2, waiting for transfers between devices, body(): lax.all_to_all(mixed, 'slab', split_axis=0, concat_axis=0, tiled=True)  99.7 us
    all_to_all x1, blocking collectives, body(): lax.all_to_all(sent[j], 'slab', split_axis=0, concat_axis=0, tiled=True)  77.3 us
    psum x1, blocking collectives, body(): summed = lax.psum(jnp.sum(sums), 'slab')  44 us
    all_to_all x1, waiting for transfers between devices, body(): lax.all_to_all(sent[j], 'slab', split_axis=0, concat_axis=0, tiled=True)  39.5 us
    pallas_call x2, Pallas kernels, body(): pl.pallas_call(middle_kernel, in_specs=[smem, smem, smem, vmem, vmem, vme...  37.1 us
    all_to_all x2, starting transfers between devices, body(): lax.all_to_all(mixed, 'slab', split_axis=0, concat_axis=0, tiled=True)  30.9 us
    pallas_call x1, Pallas kernels, body(): pl.pallas_call(tail_kernel, grid_spec=pltpu.PrefetchScalarGridSpec(num_sc...  18.5 us
    pallas_call x1, Pallas kernels, body(): pl.pallas_call(head_kernel, grid=(sites,), in_specs=[row_spec, b_spec, z_...  14.6 us
  transfers between devices with their start and end apart: 3, of which 3 were waited for; matrix products, arithmetic and copies ran while one was open for 0% of the time, Pallas kernels for 10%

profile of v1, /device:TPU:0, one launch (start us, length us, event | category | flops | bytes accessed | tf_op | source)
XLA Modules:
  0.0 376.0 jit_solution(12507042212098912364)
XLA Ops:
  0.6 14.6 %head.1 = (f32[16,12,16,256]{3,2,1,0:T(8,128)}, f32[16,12,16,256]{3,2,1,0:T(8,128)}) custom-call(f32[12,16,32,256]{3,2,1,0:T(8,128)} %refs_2_.1, bf16[2,256,256]{2,1,0:T(8,128)(2,1)} %constant.31.clone.b_ref.a_ref.refs_5_, bf16[2,256,256]{2,1,0:T(8,128)(2,1)} %constant.32.clone.z_ref), custom_call_target="tpu_custom_call" | custom-call | flops 4831838208 | bytes 12582912 | tf_op jit(solution)/shard_map/head/pallas_call | solution.py:194
  15.2 77.3 %all_to_all.20.x_ref = f32[16,12,16,256]{3,2,1,0:T(8,128)} all-to-all(f32[16,12,16,256]{3,2,1,0:T(8,128)} %get-tuple-element.8), channel_id=1, replica_groups=mesh['sys'=2,'slab'=16] {'slab'}, dimensions={0} | all-to-all | bytes 6291456 | tf_op jit(solution)/shard_map/all_to_all | solution.py:213
  92.5 0.0 copy-start.2
  92.5 0.0 copy-start.3
  92.5 5.3 %all-to-all-start.2 = ((f32[16,12,16,256]{3,2,1,0:T(8,128)}), f32[16,12,16,256]{3,2,1,0:T(8,128)S(1)}, u32[]{:S(2)}, u32[]{:S(2)}) async-start(f32[16,12,16,256]{3,2,1,0:T(8,128)} %get-tuple-element.9), calls=%async_computation.2 | async-start | bytes 6291456 | tf_op jit(solution)/shard_map/all_to_all | solution.py:213
  97.8 0.0 copy-done.2
  97.9 0.7 reshape.12.amp_ref
  98.6 0.0 copy-done.3
  98.6 0.6 fusion
  99.2 18.5 %middle.2 = f32[16,12,16,256]{3,2,1,0:T(8,128)} custom-call(f32[432]{0:T(512)} %reshape.12.amp_ref, f32[3]{0:T(128)} %width_ref.3, f32[1]{0:T(128)} %get-tuple-element.14.kz_ref, f32[16,12,16,256]{3,2,1,0:T(8,128)} %all_to_all.20.x_ref, bf16[2,256,256]{2,1,0:T(8,128)(2,1)} %constant.31.clone.b_ref.a_ref.refs_5_, f32[256,256]{1,0:T(8,128)} %constant.35.clone.ka_ref, ...), custom_call_target="tpu_custom_call" | custom-call | flops 4026531840 | bytes 6291456 | tf_op jit(solution)/shard_map/middle/pallas_call | solution.py:214
  117.7 39.5 %all-to-all-done.2.x_ref = f32[16,12,16,256]{3,2,1,0:T(8,128)S(1)} async-done(((f32[16,12,16,256]{3,2,1,0:T(8,128)}), f32[16,12,16,256]{3,2,1,0:T(8,128)S(1)}, u32[]{:S(2)}, u32[]{:S(2)}) %all-to-all-start.2) | async-done | bytes 3145760 | tf_op jit(solution)/shard_map/all_to_all | solution.py:213
  157.2 0.0 copy-start
  157.2 1.7 copy-done
  158.9 15.5 %all-to-all-start.1 = ((f32[16,12,16,256]{3,2,1,0:T(8,128)}), f32[16,12,16,256]{3,2,1,0:T(8,128)}, u32[]{:S(2)}, u32[]{:S(2)}) async-start(f32[16,12,16,256]{3,2,1,0:T(8,128)} %middle.2), calls=%async_computation.1 | async-start | bytes 6291456 | tf_op jit(solution)/shard_map/all_to_all | solution.py:226
  174.3 18.6 %middle.3 = f32[16,12,16,256]{3,2,1,0:T(8,128)} custom-call(f32[432]{0:T(512)} %reshape.12.amp_ref, f32[3]{0:T(128)} %width_ref.3, f32[1]{0:T(128)} %get-tuple-element.13.kz_ref, f32[16,12,16,256]{3,2,1,0:T(8,128)} %copy-done, bf16[2,256,256]{2,1,0:T(8,128)(2,1)} %constant.31.clone.b_ref.a_ref.refs_5_, f32[256,256]{1,0:T(8,128)} %constant.35.clone.ka_ref, ...), custom_call_target="tpu_custom_call" | custom-call | flops 4026531840 | bytes 6291456 | tf_op jit(solution)/shard_map/middle/pallas_call | solution.py:214
  192.9 0.0 copy-start.4
  192.9 40.8 %all-to-all-done.1.refs_0_ = f32[16,12,16,256]{3,2,1,0:T(8,128)} async-done(((f32[16,12,16,256]{3,2,1,0:T(8,128)}), f32[16,12,16,256]{3,2,1,0:T(8,128)}, u32[]{:S(2)}, u32[]{:S(2)}) %all-to-all-start.1) | async-done | bytes 3145760 | tf_op jit(solution)/shard_map/all_to_all | solution.py:226
  233.8 15.4 %all-to-all-start.3 = ((f32[16,12,16,256]{3,2,1,0:T(8,128)}), f32[16,12,16,256]{3,2,1,0:T(8,128)S(1)}, u32[]{:S(2)}, u32[]{:S(2)}) async-start(f32[16,12,16,256]{3,2,1,0:T(8,128)} %middle.3), calls=%async_computation.3 | async-start | bytes 6291456 | tf_op jit(solution)/shard_map/all_to_all | solution.py:226
  249.2 0.0 copy-done.4
  249.2 0.5 convert_element_type.3.charge_ref
  249.7 58.8 %all-to-all-done.3.refs_1_ = f32[16,12,16,256]{3,2,1,0:T(8,128)S(1)} async-done(((f32[16,12,16,256]{3,2,1,0:T(8,128)}), f32[16,12,16,256]{3,2,1,0:T(8,128)S(1)}, u32[]{:S(2)}, u32[]{:S(2)}) %all-to-all-start.3) | async-done | bytes 3145760 | tf_op jit(solution)/shard_map/all_to_all | solution.py:226
  308.6 0.0 copy-start.1
  308.6 1.7 copy-done.1
  310.3 18.5 %tail.1 = (f32[12,16,32,256]{3,2,1,0:T(8,128)}, f32[12,16,32,256]{3,2,1,0:T(8,128)}, f32[8,256]{1,0:T(8,128)}) custom-call(s32[12]{0:T(128)} %species_ref.1, f32[12]{0:T(128)} %convert_element_type.3.charge_ref, f32[16,12,16,256]{3,2,1,0:T(8,128)} %all-to-all-done.1.refs_0_, f32[16,12,16,256]{3,2,1,0:T(8,128)} %copy-done.1, f32[12,16,32,256]{3,2,1,0:T(8,128)} %refs_2_.1, ...), custom_call_target="tpu_custom_call" | custom-call | flops 4831838208 | bytes 31457280 | tf_op jit(solution)/shard_map/tail/pallas_call | solution.py:228
  328.8 1.3 reduce_sum.9
  330.1 44.0 %psum.7 = f32[]{:T(128)} all-reduce(f32[]{:T(128)} %reduce_sum.9), channel_id=1, replica_groups=mesh['sys'=2,'slab'=16] {'slab'}, use_global_device_ids=true, to_apply=%region_1.0 | all-reduce | flops 1 | bytes 8 | tf_op jit(solution)/shard_map/psum | solution.py:253
Async XLA Ops:
  92.5 5.3 %copy-start.2 = (f32[3,12,12]{2,1,0:T(8,128)S(1)}, f32[3,12,12]{2,1,0:T(8,128)}, u32[]{:S(2)}) copy-start(f32[3,12,12]{2,1,0:T(8,128)} %param.19) | copy-start | bytes 5188
  92.5 6.0 %copy-start.3 = (f32[32]{0:T(128)S(1)}, f32[32]{0:T(128)}, u32[]{:S(2)}) copy-start(f32[32]{0:T(128)} %constant.34.clone) | copy-start | bytes 388
  92.5 64.7 %all-to-all-start.2 = ((f32[16,12,16,256]{3,2,1,0:T(8,128)}), f32[16,12,16,256]{3,2,1,0:T(8,128)S(1)}, u32[]{:S(2)}, u32[]{:S(2)}) async-start(f32[16,12,16,256]{3,2,1,0:T(8,128)} %get-tuple-element.9), calls=%async_computation.2 | async-start | bytes 6291456 | tf_op jit(solution)/shard_map/all_to_all | solution.py:213
  157.2 1.7 copy-start
  158.9 74.9 %all-to-all-start.1 = ((f32[16,12,16,256]{3,2,1,0:T(8,128)}), f32[16,12,16,256]{3,2,1,0:T(8,128)}, u32[]{:S(2)}, u32[]{:S(2)}) async-start(f32[16,12,16,256]{3,2,1,0:T(8,128)} %middle.2), calls=%async_computation.1 | async-start | bytes 6291456 | tf_op jit(solution)/shard_map/all_to_all | solution.py:226
  192.9 56.3 %copy-start.4 = (s32[12]{0:T(128)S(1)}, s32[12]{0:T(128)}, u32[]{:S(2)}) copy-start(s32[12]{0:T(128)} %param.18) | copy-start | bytes 148
  233.8 74.8 %all-to-all-start.3 = ((f32[16,12,16,256]{3,2,1,0:T(8,128)}), f32[16,12,16,256]{3,2,1,0:T(8,128)S(1)}, u32[]{:S(2)}, u32[]{:S(2)}) async-start(f32[16,12,16,256]{3,2,1,0:T(8,128)} %middle.3), calls=%async_computation.3 | async-start | bytes 6291456 | tf_op jit(solution)/shard_map/all_to_all | solution.py:226
  308.6 1.7 copy-start.1

commit v2 on v1

--- a/solution.py
+++ b/solution.py
@@ -116,6 +116,34 @@
         total_ref[0, here] = total
         next_ref[0, here] = after
         sum_ref[...] += jnp.sum((change * change).reshape(-1, 8, columns), axis=0)
+
+
+def gather_kernel(sum_ref, out_ref, mine_ref, slots_ref, send_sem, recv_sem):
+    devices = slots_ref.shape[0]
+    me = lax.axis_index("slab")
+    barrier = pltpu.get_barrier_semaphore()
+    for i in range(1, devices):
+        pl.semaphore_signal(barrier, inc=1, device_id={"slab": lax.rem(me + i, devices)})
+    total = sum_ref[:, :128]
+    for i in range(1, sum_ref.shape[1] // 128):
+        total = total + sum_ref[:, i * 128:(i + 1) * 128]
+    mine_ref[...] = total
+    slots_ref[me] = total
+    pl.semaphore_wait(barrier, devices - 1)
+    copies = []
+    for i in range(1, devices):
+        copy = pltpu.make_async_remote_copy(
+            src_ref=mine_ref,
+            dst_ref=slots_ref.at[me],
+            send_sem=send_sem.at[i],
+            recv_sem=recv_sem.at[i],
+            device_id={"slab": lax.rem(me + i, devices)},
+        )
+        copy.start()
+        copies.append(copy)
+    for copy in copies:
+        copy.wait()
+    out_ref[...] = jnp.sum(slots_ref[...], axis=0)
 
 
 def plain_mix(values, square, chi_amp, chi_width):
@@ -250,7 +278,21 @@
         ),
         name="tail",
     )(species, charges.astype(f32), *arrived, correlation, lj_field, potential, b_table, z_back)
-    summed = lax.psum(jnp.sum(sums), "slab")
+    gathered = pl.pallas_call(
+        gather_kernel,
+        in_specs=[vmem],
+        out_specs=vmem,
+        out_shape=jax.ShapeDtypeStruct((8, 128), f32),
+        scratch_shapes=[
+            pltpu.VMEM((8, 128), f32),
+            pltpu.VMEM((devices, 8, 128), f32),
+            pltpu.SemaphoreType.DMA((devices,)),
+            pltpu.SemaphoreType.DMA((devices,)),
+        ],
+        compiler_params=pltpu.CompilerParams(collective_id=0, has_side_effects=True),
+        name="gather",
+    )(sums)
+    summed = jnp.sum(gathered)
     return (total_corr, next_corr, jnp.sqrt(summed / cells + 1e-06).reshape(1))
 
 

time: 377 us -> 352 us (0.934)
  blocking collectives: 121 us -> 77.3 us
  Pallas kernels: 70.3 us -> 89.3 us
    psum x1 -> x0, blocking collectives: 44 us -> none  [body(): summed = lax.psum(jnp.sum(sums), 'slab')]
    pallas_call x0 -> x1, Pallas kernels: none -> 19.2 us  [body(): pl.pallas_call(gather_kernel, in_specs=[vmem], out_specs=vmem, out_shape=...]
  transfers between devices with their start and end apart: 3 -> 3, of which waited for: 3 -> 3; matrix products, arithmetic and copies ran while one was open for 0% -> 1% of each run, Pallas kernels for 10% -> 11%
where the time goes in v2:
time: 352 us; the launch traced here: 351 us
  waiting for transfers between devices  139 us (39%)
  Pallas kernels  89.3 us (25%)
  blocking collectives  77.3 us (22%)
  starting transfers between devices  36.2 us (10%)
  local copies, waits for them, and re-layouts  4.69 us (1%)
    all_to_all x2, waiting for transfers between devices, body(): lax.all_to_all(mixed, 'slab', split_axis=0, concat_axis=0, tiled=True)  99.7 us
    all_to_all x1, blocking collectives, body(): lax.all_to_all(sent[j], 'slab', split_axis=0, concat_axis=0, tiled=True)  77.3 us
    all_to_all x1, waiting for transfers between devices, body(): lax.all_to_all(sent[j], 'slab', split_axis=0, concat_axis=0, tiled=True)  39.5 us
    pallas_call x2, Pallas kernels, body(): pl.pallas_call(middle_kernel, in_specs=[smem, smem, smem, vmem, vmem, vme...  37.1 us
    all_to_all x2, starting transfers between devices, body(): lax.all_to_all(mixed, 'slab', split_axis=0, concat_axis=0, tiled=True)  30.9 us
    pallas_call x1, Pallas kernels, body(): pl.pallas_call(gather_kernel, in_specs=[vmem], out_specs=vmem, out_shape=...  19.2 us
    pallas_call x1, Pallas kernels, body(): pl.pallas_call(tail_kernel, grid_spec=pltpu.PrefetchScalarGridSpec(num_sc...  18.4 us
    pallas_call x1, Pallas kernels, body(): pl.pallas_call(head_kernel, grid=(sites,), in_specs=[row_spec, b_spec, z_...  14.6 us
  transfers between devices with their start and end apart: 3, of which 3 were waited for; matrix products, arithmetic and copies ran while one was open for 1% of the time, Pallas kernels for 11%

profile of v2, /device:TPU:0, one launch (start us, length us, event | category | flops | bytes accessed | tf_op | source)
XLA Modules:
  0.0 350.9 jit_solution(2538456067108064052)
XLA Ops:
  0.6 14.6 %head.1 = (f32[16,12,16,256]{3,2,1,0:T(8,128)}, f32[16,12,16,256]{3,2,1,0:T(8,128)}) custom-call(f32[12,16,32,256]{3,2,1,0:T(8,128)} %refs_2_.1, bf16[2,256,256]{2,1,0:T(8,128)(2,1)} %constant.31.clone.b_ref.a_ref.refs_5_, bf16[2,256,256]{2,1,0:T(8,128)(2,1)} %constant.32.clone.z_ref), custom_call_target="tpu_custom_call" | custom-call | flops 4831838208 | bytes 12582912 | tf_op jit(solution)/shard_map/head/pallas_call | solution.py:222
  15.2 77.3 %all_to_all.20.x_ref = f32[16,12,16,256]{3,2,1,0:T(8,128)} all-to-all(f32[16,12,16,256]{3,2,1,0:T(8,128)} %get-tuple-element.8), channel_id=1, replica_groups=mesh['sys'=2,'slab'=16] {'slab'}, dimensions={0} | all-to-all | bytes 6291456 | tf_op jit(solution)/shard_map/all_to_all | solution.py:241
  92.5 0.0 copy-start.2
  92.5 0.0 copy-start.3
  92.5 5.3 %all-to-all-start.2 = ((f32[16,12,16,256]{3,2,1,0:T(8,128)}), f32[16,12,16,256]{3,2,1,0:T(8,128)S(1)}, u32[]{:S(2)}, u32[]{:S(2)}) async-start(f32[16,12,16,256]{3,2,1,0:T(8,128)} %get-tuple-element.9), calls=%async_computation.2 | async-start | bytes 6291456 | tf_op jit(solution)/shard_map/all_to_all | solution.py:241
  97.8 0.0 copy-done.2
  97.9 0.7 reshape.12.amp_ref
  98.5 0.0 copy-done.3
  98.5 0.7 fusion
  99.2 18.5 %middle.2 = f32[16,12,16,256]{3,2,1,0:T(8,128)} custom-call(f32[432]{0:T(512)} %reshape.12.amp_ref, f32[3]{0:T(128)} %width_ref.3, f32[1]{0:T(128)} %get-tuple-element.14.kz_ref, f32[16,12,16,256]{3,2,1,0:T(8,128)} %all_to_all.20.x_ref, bf16[2,256,256]{2,1,0:T(8,128)(2,1)} %constant.31.clone.b_ref.a_ref.refs_5_, f32[256,256]{1,0:T(8,128)} %constant.35.clone.ka_ref, ...), custom_call_target="tpu_custom_call" | custom-call | flops 4026531840 | bytes 6291456 | tf_op jit(solution)/shard_map/middle/pallas_call | solution.py:242
  117.7 39.5 %all-to-all-done.2.x_ref = f32[16,12,16,256]{3,2,1,0:T(8,128)S(1)} async-done(((f32[16,12,16,256]{3,2,1,0:T(8,128)}), f32[16,12,16,256]{3,2,1,0:T(8,128)S(1)}, u32[]{:S(2)}, u32[]{:S(2)}) %all-to-all-start.2) | async-done | bytes 3145760 | tf_op jit(solution)/shard_map/all_to_all | solution.py:241
  157.2 0.0 copy-start
  157.2 1.7 copy-done
  158.9 15.5 %all-to-all-start.1 = ((f32[16,12,16,256]{3,2,1,0:T(8,128)}), f32[16,12,16,256]{3,2,1,0:T(8,128)}, u32[]{:S(2)}, u32[]{:S(2)}) async-start(f32[16,12,16,256]{3,2,1,0:T(8,128)} %middle.2), calls=%async_computation.1 | async-start | bytes 6291456 | tf_op jit(solution)/shard_map/all_to_all | solution.py:254
  174.3 18.6 %middle.3 = f32[16,12,16,256]{3,2,1,0:T(8,128)} custom-call(f32[432]{0:T(512)} %reshape.12.amp_ref, f32[3]{0:T(128)} %width_ref.3, f32[1]{0:T(128)} %get-tuple-element.13.kz_ref, f32[16,12,16,256]{3,2,1,0:T(8,128)} %copy-done, bf16[2,256,256]{2,1,0:T(8,128)(2,1)} %constant.31.clone.b_ref.a_ref.refs_5_, f32[256,256]{1,0:T(8,128)} %constant.35.clone.ka_ref, ...), custom_call_target="tpu_custom_call" | custom-call | flops 4026531840 | bytes 6291456 | tf_op jit(solution)/shard_map/middle/pallas_call | solution.py:242
  192.9 0.0 copy-start.4
  192.9 40.9 %all-to-all-done.1.refs_0_ = f32[16,12,16,256]{3,2,1,0:T(8,128)} async-done(((f32[16,12,16,256]{3,2,1,0:T(8,128)}), f32[16,12,16,256]{3,2,1,0:T(8,128)}, u32[]{:S(2)}, u32[]{:S(2)}) %all-to-all-start.1) | async-done | bytes 3145760 | tf_op jit(solution)/shard_map/all_to_all | solution.py:254
  233.8 15.4 %all-to-all-start.3 = ((f32[16,12,16,256]{3,2,1,0:T(8,128)}), f32[16,12,16,256]{3,2,1,0:T(8,128)S(1)}, u32[]{:S(2)}, u32[]{:S(2)}) async-start(f32[16,12,16,256]{3,2,1,0:T(8,128)} %middle.3), calls=%async_computation.3 | async-start | bytes 6291456 | tf_op jit(solution)/shard_map/all_to_all | solution.py:254
  249.2 0.0 copy-done.4
  249.2 0.5 convert_element_type.3.charge_ref
  249.7 58.8 %all-to-all-done.3.refs_1_ = f32[16,12,16,256]{3,2,1,0:T(8,128)S(1)} async-done(((f32[16,12,16,256]{3,2,1,0:T(8,128)}), f32[16,12,16,256]{3,2,1,0:T(8,128)S(1)}, u32[]{:S(2)}, u32[]{:S(2)}) %all-to-all-start.3) | async-done | bytes 3145760 | tf_op jit(solution)/shard_map/all_to_all | solution.py:254
  308.6 0.0 copy-start.1
  308.6 1.7 copy-done.1
  310.2 18.4 %tail.1 = (f32[12,16,32,256]{3,2,1,0:T(8,128)}, f32[12,16,32,256]{3,2,1,0:T(8,128)}, f32[8,256]{1,0:T(8,128)}) custom-call(s32[12]{0:T(128)} %species_ref.1, f32[12]{0:T(128)} %convert_element_type.3.charge_ref, f32[16,12,16,256]{3,2,1,0:T(8,128)} %all-to-all-done.1.refs_0_, f32[16,12,16,256]{3,2,1,0:T(8,128)} %copy-done.1, f32[12,16,32,256]{3,2,1,0:T(8,128)} %refs_2_.1, ...), custom_call_target="tpu_custom_call" | custom-call | flops 4831838208 | bytes 31457280 | tf_op jit(solution)/shard_map/tail/pallas_call | solution.py:256
  328.7 19.2 %gather.1 = f32[8,128]{1,0:T(8,128)} custom-call(f32[8,256]{1,0:T(8,128)} %get-tuple-element.12.sum_ref), custom_call_target="tpu_custom_call" | custom-call | tf_op jit(solution)/shard_map/gather/pallas_call | solution.py:281
  347.8 1.3 reduce_sum.9
Async XLA Ops:
  92.5 5.3 %copy-start.2 = (f32[3,12,12]{2,1,0:T(8,128)S(1)}, f32[3,12,12]{2,1,0:T(8,128)}, u32[]{:S(2)}) copy-start(f32[3,12,12]{2,1,0:T(8,128)} %param.19) | copy-start | bytes 5188
  92.5 6.0 %copy-start.3 = (f32[32]{0:T(128)S(1)}, f32[32]{0:T(128)}, u32[]{:S(2)}) copy-start(f32[32]{0:T(128)} %constant.34.clone) | copy-start | bytes 388
  92.5 64.7 %all-to-all-start.2 = ((f32[16,12,16,256]{3,2,1,0:T(8,128)}), f32[16,12,16,256]{3,2,1,0:T(8,128)S(1)}, u32[]{:S(2)}, u32[]{:S(2)}) async-start(f32[16,12,16,256]{3,2,1,0:T(8,128)} %get-tuple-element.9), calls=%async_computation.2 | async-start | bytes 6291456 | tf_op jit(solution)/shard_map/all_to_all | solution.py:241
  157.2 1.7 copy-start
  158.9 74.9 %all-to-all-start.1 = ((f32[16,12,16,256]{3,2,1,0:T(8,128)}), f32[16,12,16,256]{3,2,1,0:T(8,128)}, u32[]{:S(2)}, u32[]{:S(2)}) async-start(f32[16,12,16,256]{3,2,1,0:T(8,128)} %middle.2), calls=%async_computation.1 | async-start | bytes 6291456 | tf_op jit(solution)/shard_map/all_to_all | solution.py:254
  192.9 56.3 %copy-start.4 = (s32[12]{0:T(128)S(1)}, s32[12]{0:T(128)}, u32[]{:S(2)}) copy-start(s32[12]{0:T(128)} %param.18) | copy-start | bytes 148
  233.8 74.8 %all-to-all-start.3 = ((f32[16,12,16,256]{3,2,1,0:T(8,128)}), f32[16,12,16,256]{3,2,1,0:T(8,128)S(1)}, u32[]{:S(2)}, u32[]{:S(2)}) async-start(f32[16,12,16,256]{3,2,1,0:T(8,128)} %middle.3), calls=%async_computation.3 | async-start | bytes 6291456 | tf_op jit(solution)/shard_map/all_to_all | solution.py:254
  308.6 1.7 copy-start.1

commit v3 on v2

--- a/solution.py
+++ b/solution.py
@@ -52,50 +52,133 @@
     return mul(high, table[0]) + (mul(low, table[0]) + mul(high, table[1]))
 
 
-def head_kernel(x_ref, b_ref, z_ref, *outs):
-    rows, depth, columns = x_ref.shape[1:]
-    devices = outs[0].shape[0]
-    group = z_ref.shape[1] // depth
-    for i in range(rows // group):
-        part = x_ref[0, i * group:(i + 1) * group].reshape(group * depth, columns)
-        turned = left_by(z_ref, right_by(part, b_ref)).reshape(depth, group, columns)
-        for j, out in enumerate(outs):
-            out[:, 0, i * group:(i + 1) * group, :] = turned[j * devices:(j + 1) * devices]
-
-
-def middle_kernel(amp_ref, width_ref, kz_ref, x_ref, a_ref, ka_ref, kb_ref, out_ref, work_ref):
-    devices, sites, rows, columns = x_ref.shape
+def core_kernel(
+    amp_ref, width_ref, kz_ref, x_ref, b_ref, z_ref, a_ref, ka_ref, kb_ref, out_ref,
+    sent_ref, got_ref, work_ref, back_ref, send_sem, recv_sem, back_send, back_recv, own_sem,
+):
+    sites, rows, depth, columns = x_ref.shape
+    chunks, devices = sent_ref.shape[:2]
     terms = width_ref.shape[0]
     extent = devices * rows
-    for s in range(sites):
-        work_ref[s] = left_by(a_ref, x_ref[:, s].reshape(extent, columns))
-
-    @pl.loop(0, extent // 8)
-    def _(step):
-        here = pl.ds(pl.multiple_of(step * 8, 8), 8)
-        square = ka_ref[here, :] + kb_ref[...] + kz_ref[0]
-        weights = [jnp.exp(-width_ref[m] * square) for m in range(terms)]
-        values = [work_ref[t, here, :] for t in range(sites)]
-        for s in range(sites):
-            total = values[s]
-            for t in range(sites):
-                factor = amp_ref[s * sites + t] * weights[0]
-                for m in range(1, terms):
-                    factor = factor + amp_ref[(m * sites + s) * sites + t] * weights[m]
-                total = total + factor * values[t]
-            work_ref[s, here, :] = total
-
-    for s in range(sites):
-        out_ref[:, s] = left_by(a_ref, work_ref[s]).reshape(devices, rows, columns)
+    group = z_ref.shape[1] // depth
+    batches = send_sem.shape[1]
+    batch = sites // batches
+    me = lax.axis_index("slab")
+
+    def spread(j, g, i):
+        peer = lax.rem(me + i, devices)
+        own = pl.ds(g * batch, batch)
+        return pltpu.make_async_remote_copy(
+            src_ref=sent_ref.at[j, peer, own],
+            dst_ref=got_ref.at[j, me, own],
+            send_sem=send_sem.at[j, g, i],
+            recv_sem=recv_sem.at[j, g, i],
+            device_id={"slab": peer},
+        )
+
+    def restore(j, g, i):
+        peer = lax.rem(me + i, devices)
+        own = pl.ds(g * batch, batch)
+        return pltpu.make_async_remote_copy(
+            src_ref=back_ref.at[j, peer, own],
+            dst_ref=out_ref.at[j, me, own],
+            send_sem=back_send.at[j, g, i],
+            recv_sem=back_recv.at[j, g, i],
+            device_id={"slab": peer},
+        )
+
+    def keep(j):
+        return pltpu.make_async_copy(back_ref.at[j, me], out_ref.at[j, me], own_sem.at[j])
+
+    barrier = pltpu.get_barrier_semaphore()
+
+    @pl.loop(1, devices)
+    def _(i):
+        pl.semaphore_signal(barrier, inc=1, device_id={"slab": lax.rem(me + i, devices)})
+
+    pl.semaphore_wait(barrier, devices - 1)
+
+    @pl.loop(0, batches)
+    def _(g):
+        for k in range(batch):
+            s = g * batch + k
+            for r in range(rows // group):
+                here = slice(r * group, (r + 1) * group)
+                part = x_ref[s, here].reshape(group * depth, columns)
+                turned = left_by(z_ref, right_by(part, b_ref)).reshape(depth, group, columns)
+                for j in range(chunks):
+                    sent_ref[j, :, s, here, :] = turned[j * devices:(j + 1) * devices]
+
+        @pl.loop(1, devices)
+        def _(i):
+            spread(0, g, i).start()
+
+    @pl.loop(1, chunks)
+    def _(j):
+        @pl.loop(0, batches)
+        def _(g):
+            @pl.loop(1, devices)
+            def _(i):
+                spread(j, g, i).start()
+
+    @pl.loop(0, chunks)
+    def _(j):
+        got_ref[j, me] = sent_ref[j, me]
+
+        @pl.loop(0, batches)
+        def _(g):
+            @pl.loop(1, devices)
+            def _(i):
+                spread(j, g, i).wait_recv()
+
+            for k in range(batch):
+                s = g * batch + k
+                work_ref[s] = left_by(a_ref, got_ref[j, :, s].reshape(extent, columns))
+
+        @pl.loop(0, extent // 8)
+        def _(step):
+            here = pl.ds(pl.multiple_of(step * 8, 8), 8)
+            square = ka_ref[here, :] + kb_ref[...] + kz_ref[j * devices + me]
+            weights = [jnp.exp(-width_ref[m] * square) for m in range(terms)]
+            values = [work_ref[t, here, :] for t in range(sites)]
+            for s in range(sites):
+                total = values[s]
+                for t in range(sites):
+                    factor = amp_ref[s * sites + t] * weights[0]
+                    for m in range(1, terms):
+                        factor = factor + amp_ref[(m * sites + s) * sites + t] * weights[m]
+                    total = total + factor * values[t]
+                work_ref[s, here, :] = total
+
+        @pl.loop(0, batches)
+        def _(g):
+            for k in range(batch):
+                s = g * batch + k
+                back_ref[j, :, s] = left_by(a_ref, work_ref[s]).reshape(devices, rows, columns)
+
+            @pl.loop(1, devices)
+            def _(i):
+                restore(j, g, i).start()
+
+        keep(j).start()
+
+    @pl.loop(0, chunks)
+    def _(j):
+        keep(j).wait()
+
+        @pl.loop(0, batches)
+        def _(g):
+            @pl.loop(1, devices)
+            def _(i):
+                spread(j, g, i).wait_send()
+                restore(j, g, i).wait()
 
 
 def tail_kernel(species_ref, charge_ref, *refs):
-    count = len(refs) - 8
-    parts = refs[:count]
-    x_ref, lj_ref, pot_ref, b_ref, z_ref, total_ref, next_ref, sum_ref = refs[count:]
+    parts_ref, x_ref, lj_ref, pot_ref, b_ref, z_ref, total_ref, next_ref, sum_ref = refs
     site = pl.program_id(0)
     rows, depth, columns = x_ref.shape[1:]
-    devices = parts[0].shape[0]
+    chunks, devices = parts_ref.shape[:2]
     group = z_ref.shape[1] // depth
 
     @pl.when(site == 0)
@@ -105,8 +188,7 @@
     charge = charge_ref[site]
     for i in range(rows // group):
         here = slice(i * group, (i + 1) * group)
-        blocks = [part[:, 0, here, :].reshape(devices * group, columns) for part in parts]
-        joined = jnp.concatenate(blocks, axis=0) if count > 1 else blocks[0]
+        joined = parts_ref[:, :, 0, here, :].reshape(chunks * devices * group, columns)
         total = right_by(left_by(z_ref, joined), b_ref).reshape(group, depth, columns)
         before = x_ref[0, here]
         indirect = total - before
@@ -215,50 +297,46 @@
     b_spec = pl.BlockSpec((2, columns, columns), lambda s, *_: (0, 0, 0))
     z_spec = pl.BlockSpec((2, group * depth, group * depth), lambda s, *_: (0, 0, 0))
     row_spec = pl.BlockSpec((1, rows, depth, columns), lambda s, *_: (s, 0, 0, 0))
-    part_spec = pl.BlockSpec((devices, 1, rows, columns), lambda s, *_: (0, s, 0, 0))
-    part_shape = jax.ShapeDtypeStruct((devices, sites, rows, columns), f32)
+    part_spec = pl.BlockSpec(
+        (chunks, devices, 1, rows, columns), lambda s, *_: (0, 0, s, 0, 0)
+    )
+    whole = (chunks, devices, sites, rows, columns)
     size = correlation.size
-
-    sent = pl.pallas_call(
-        head_kernel,
-        grid=(sites,),
-        in_specs=[row_spec, b_spec, z_spec],
-        out_specs=[part_spec] * chunks,
-        out_shape=[part_shape] * chunks,
-        compiler_params=pltpu.CompilerParams(vmem_limit_bytes=limit),
-        cost_estimate=pl.CostEstimate(
-            flops=12 * size * columns, bytes_accessed=8 * size, transcendentals=0
-        ),
-        name="head",
-    )(correlation, b_table, z_table)
+    batches = 4 if sites % 4 == 0 else 1
+    pairs = pltpu.SemaphoreType.DMA((chunks, batches, devices))
 
     kz = jnp.asarray(signed_square(depth))
     ka = jnp.asarray(np.repeat(signed_square(extent)[:, None], columns, axis=1))
     kb = jnp.asarray(np.repeat(signed_square(columns)[None, :], 8, axis=0))
-    amp = chi_amp.reshape(-1)
-    arrived = []
-    for j in range(chunks):
-        got = lax.all_to_all(sent[j], "slab", split_axis=0, concat_axis=0, tiled=True)
-        mixed = pl.pallas_call(
-            middle_kernel,
-            in_specs=[smem, smem, smem, vmem, vmem, vmem, vmem],
-            out_specs=vmem,
-            out_shape=part_shape,
-            scratch_shapes=[pltpu.VMEM((sites, extent, columns), f32)],
-            compiler_params=pltpu.CompilerParams(vmem_limit_bytes=limit),
-            cost_estimate=pl.CostEstimate(
-                flops=20 * size * extent // chunks, bytes_accessed=8 * size // chunks, transcendentals=0
-            ),
-            name="middle",
-        )(amp, chi_width, lax.dynamic_slice(kz, (j * devices + me,), (1,)), got, a_table, ka, kb)
-        arrived.append(lax.all_to_all(mixed, "slab", split_axis=0, concat_axis=0, tiled=True))
+    arrived = pl.pallas_call(
+        core_kernel,
+        in_specs=[smem, smem, smem] + [vmem] * 6,
+        out_specs=pl.BlockSpec(memory_space=pl.ANY),
+        out_shape=jax.ShapeDtypeStruct(whole, f32),
+        scratch_shapes=[
+            pltpu.VMEM(whole, f32),
+            pltpu.VMEM(whole, f32),
+            pltpu.VMEM((sites, extent, columns), f32),
+            pltpu.VMEM(whole, f32),
+            pairs,
+            pairs,
+            pairs,
+            pairs,
+            pltpu.SemaphoreType.DMA((chunks,)),
+        ],
+        compiler_params=pltpu.CompilerParams(
+            collective_id=1, has_side_effects=True, vmem_limit_bytes=limit
+        ),
+        name="core",
+    )(chi_amp.reshape(-1), chi_width, kz, correlation, b_table, z_table, a_table, ka, kb)
 
     total_corr, next_corr, sums = pl.pallas_call(
         tail_kernel,
         grid_spec=pltpu.PrefetchScalarGridSpec(
             num_scalar_prefetch=2,
             grid=(sites,),
-            in_specs=[part_spec] * chunks + [
+            in_specs=[
+                part_spec,
                 row_spec,
                 pl.BlockSpec((1, rows, depth, columns), lambda s, kind, _: (kind[s], 0, 0, 0)),
                 pl.BlockSpec((rows, depth, columns), lambda s, *_: (0, 0, 0)),
@@ -277,7 +355,7 @@
             flops=12 * size * columns, bytes_accessed=20 * size, transcendentals=size
         ),
         name="tail",
-    )(species, charges.astype(f32), *arrived, correlation, lj_field, potential, b_table, z_back)
+    )(species, charges.astype(f32), arrived, correlation, lj_field, potential, b_table, z_back)
     gathered = pl.pallas_call(
         gather_kernel,
         in_specs=[vmem],

time: 352 us -> 320 us (0.909)
  Pallas kernels: 89.3 us -> 313 us
  waiting for transfers between devices: 139 us -> 0 us
  blocking collectives: 77.3 us -> 0 us
  starting transfers between devices: 36.2 us -> 0 us
    pallas_call x3 -> x1, Pallas kernels: 51.7 us -> 281 us  [body(): pl.pallas_call(core_kernel, in_specs=[smem, smem, smem] + [vmem] * 6, out...]
    all_to_all x3 -> x0, waiting for transfers between devices: 139 us -> none  [the longest x2 99.7 us: body(): lax.all_to_all(mixed, 'slab', split_axis=0, concat_axis=0, tiled=True)]
    all_to_all x1 -> x0, blocking collectives: 77.3 us -> none  [body(): lax.all_to_all(sent[j], 'slab', split_axis=0, concat_axis=0, tiled=True)]
    all_to_all x3 -> x0, starting transfers between devices: 36.2 us -> none  [the longest x2 30.9 us: body(): lax.all_to_all(mixed, 'slab', split_axis=0, concat_axis=0, tiled=True)]
    pallas_call x1, Pallas kernels: 19.2 us -> 13.8 us  [body(): pl.pallas_call(gather_kernel, in_specs=[vmem], out_specs=vmem, out_shape=...]
  transfers between devices with their start and end apart: 3 -> 0, of which waited for: 3 -> 0; matrix products, arithmetic and copies ran while one was open for 1% -> 0% of each run, Pallas kernels for 11% -> 0%
where the time goes in v3:
time: 320 us; the launch traced here: 319 us
  Pallas kernels  313 us (98%)
    pallas_call x1, Pallas kernels, body(): pl.pallas_call(core_kernel, in_specs=[smem, smem, smem] + [vmem] * 6, out...  281 us
    pallas_call x1, Pallas kernels, body(): pl.pallas_call(tail_kernel, grid_spec=pltpu.PrefetchScalarGridSpec(num_sc...  18.4 us
    pallas_call x1, Pallas kernels, body(): pl.pallas_call(gather_kernel, in_specs=[vmem], out_specs=vmem, out_shape=...  13.8 us

profile of v3, /device:TPU:0, one launch (start us, length us, event | category | flops | bytes accessed | tf_op | source)
XLA Modules:
  0.0 319.5 jit_solution(9409808154768921109)
XLA Ops:
  0.6 1.2 convert_element_type.3.charge_ref
  1.8 1.4 reshape.12.amp_ref
  3.2 280.9 %core.1.refs_0_ = f32[2,16,12,16,256]{4,3,2,1,0:T(8,128)} custom-call(f32[432]{0:T(512)} %reshape.12.amp_ref, f32[3]{0:T(128)} %width_ref.1, f32[32]{0:T(128)} %constant.22.clone.kz_ref, f32[12,16,32,256]{3,2,1,0:T(8,128)} %refs_1_.1, bf16[2,256,256]{2,1,0:T(8,128)(2,1)} %constant.19.clone.b_ref.a_ref.refs_4_, bf16[2,256,256]{2,1,0:T(8,128)(2,1)} %constant.20.clone.z_ref, ...), custom_call_target="tpu_custom_call" | custom-call | tf_op jit(solution)/shard_map/core/pallas_call | solution.py:311
  284.1 18.4 %tail.1 = (f32[12,16,32,256]{3,2,1,0:T(8,128)}, f32[12,16,32,256]{3,2,1,0:T(8,128)}, f32[8,256]{1,0:T(8,128)}) custom-call(s32[12]{0:T(128)} %species_ref.1, f32[12]{0:T(128)} %convert_element_type.3.charge_ref, f32[2,16,12,16,256]{4,3,2,1,0:T(8,128)} %core.1.refs_0_, f32[12,16,32,256]{3,2,1,0:T(8,128)} %refs_1_.1, f32[6,16,32,256]{3,2,1,0:T(8,128)} %refs_2_.1, ...), custom_call_target="tpu_custom_call" | custom-call | flops 4831838208 | bytes 31457280 | tf_op jit(solution)/shard_map/tail/pallas_call | solution.py:333
  302.5 13.8 %gather.1 = f32[8,128]{1,0:T(8,128)} custom-call(f32[8,256]{1,0:T(8,128)} %get-tuple-element.8.sum_ref), custom_call_target="tpu_custom_call" | custom-call | tf_op jit(solution)/shard_map/gather/pallas_call | solution.py:359
  316.4 1.3 reduce_sum.9

commit v4 on v3

--- a/solution.py
+++ b/solution.py
@@ -66,7 +66,7 @@
     me = lax.axis_index("slab")
 
     def spread(j, g, i):
-        peer = lax.rem(me + i, devices)
+        peer = lax.rem(me + 1 + lax.rem(i + devices // 2 - 2, devices - 1), devices)
         own = pl.ds(g * batch, batch)
         return pltpu.make_async_remote_copy(
             src_ref=sent_ref.at[j, peer, own],
@@ -77,7 +77,7 @@
         )
 
     def restore(j, g, i):
-        peer = lax.rem(me + i, devices)
+        peer = lax.rem(me + 1 + lax.rem(i + devices // 2 - 2, devices - 1), devices)
         own = pl.ds(g * batch, batch)
         return pltpu.make_async_remote_copy(
             src_ref=back_ref.at[j, peer, own],

time: 320 us -> 320 us (level)
    pallas_call x1, Pallas kernels: 281 us -> 287 us  [body(): pl.pallas_call(core_kernel, in_specs=[smem, smem, smem] + [vmem] * 6, out...]
    pallas_call x1, Pallas kernels: 13.8 us -> 7.94 us  [body(): pl.pallas_call(gather_kernel, in_specs=[vmem], out_specs=vmem, out_shape=...]
where the time goes in v4:
time: 320 us
  Pallas kernels  313 us (98%)
    pallas_call x1, Pallas kernels, body(): pl.pallas_call(core_kernel, in_specs=[smem, smem, smem] + [vmem] * 6, out...  287 us
    pallas_call x1, Pallas kernels, body(): pl.pallas_call(tail_kernel, grid_spec=pltpu.PrefetchScalarGridSpec(num_sc...  18.3 us
    pallas_call x1, Pallas kernels, body(): pl.pallas_call(gather_kernel, in_specs=[vmem], out_specs=vmem, out_shape=...  7.94 us

profile of v4, /device:TPU:0, one launch (start us, length us, event | category | flops | bytes accessed | tf_op | source)
XLA Modules:
  0.0 319.6 jit_solution(3324988708106949850)
XLA Ops:
  0.6 1.2 convert_element_type.3.charge_ref
  1.8 1.4 reshape.12.amp_ref
  3.2 286.9 %core.1.refs_0_ = f32[2,16,12,16,256]{4,3,2,1,0:T(8,128)} custom-call(f32[432]{0:T(512)} %reshape.12.amp_ref, f32[3]{0:T(128)} %width_ref.1, f32[32]{0:T(128)} %constant.22.clone.kz_ref, f32[12,16,32,256]{3,2,1,0:T(8,128)} %refs_1_.1, bf16[2,256,256]{2,1,0:T(8,128)(2,1)} %constant.19.clone.b_ref.a_ref.refs_4_, bf16[2,256,256]{2,1,0:T(8,128)(2,1)} %constant.20.clone.z_ref, ...), custom_call_target="tpu_custom_call" | custom-call | tf_op jit(solution)/shard_map/core/pallas_call | solution.py:311
  290.2 18.3 %tail.1 = (f32[12,16,32,256]{3,2,1,0:T(8,128)}, f32[12,16,32,256]{3,2,1,0:T(8,128)}, f32[8,256]{1,0:T(8,128)}) custom-call(s32[12]{0:T(128)} %species_ref.1, f32[12]{0:T(128)} %convert_element_type.3.charge_ref, f32[2,16,12,16,256]{4,3,2,1,0:T(8,128)} %core.1.refs_0_, f32[12,16,32,256]{3,2,1,0:T(8,128)} %refs_1_.1, f32[6,16,32,256]{3,2,1,0:T(8,128)} %refs_2_.1, ...), custom_call_target="tpu_custom_call" | custom-call | flops 4831838208 | bytes 31457280 | tf_op jit(solution)/shard_map/tail/pallas_call | solution.py:333
  308.5 7.9 %gather.1 = f32[8,128]{1,0:T(8,128)} custom-call(f32[8,256]{1,0:T(8,128)} %get-tuple-element.8.sum_ref), custom_call_target="tpu_custom_call" | custom-call | tf_op jit(solution)/shard_map/gather/pallas_call | solution.py:359
  316.4 1.3 reduce_sum.9
